TPU v7x, 256 devices: a whole 4x4x8 slice. The times are simulated.
256 devices in a mesh: leaf: 256 (over y, x, z, core).
Axes of the slice: x: 4, y: 4, z: 8, core: 2. Of those that a mesh axis runs over, the one named last changes fastest.
Arguments:
- coords: float32 [16, 1048576], P(None, 'leaf'), may hold values from -128 to 128
- solution: float32 [16, 1048576], P(None, 'leaf'), may hold values from -6 to 6
- residual: float32 [16, 1048576], P(None, 'leaf'), may hold values from -128 to 128
- direction: float32 [16, 1048576], P(None, 'leaf'), may hold values from -128 to 128
- order: int32 [1048576], P('leaf'), may hold values from 0 to 4095, as said below
- leaf_skel: int32 [512, 256], P('leaf'), may hold values from 0 to 2047, as said below
- local_skel: int32 [256, 256], P('leaf'), may hold values from 0 to 511, as said below
- upper_skel: int32 [7, 256, 256], P(None, 'leaf'), may hold values from 0 to 511, as said below
Outputs:
- new_solution: float32 [16, 1048576], P(None, 'leaf')
- new_residual: float32 [16, 1048576], P(None, 'leaf')
- new_direction: float32 [16, 1048576], P(None, 'leaf')
Inputs may be any that keep to these rules, and one draw needn't show every extreme that they name: `order`: each device's block of 4096 entries is a permutation of 0 to 4095. `leaf_skel`: the 256 entries of a row are distinct. `local_skel`: the 256 entries of a row are distinct. `upper_skel`: the 256 entries of a row are distinct; for each u, the rows of devices whose indices agree after dropping the lowest u + 1 bits are equal.
All inputs are finite; a program needn't handle non-finite values.
Results may differ from a plain program's by a relative error of at most 0.0003.
Values sent between devices are 32-bit elements; how exact they have to be, the bound alone decides.
A program may use at most 320 MiB of HBM per device.

v0:
```python
import jax
import jax.numpy as jnp
from jax import lax
from jax.sharding import PartitionSpec as P

ITERS = 4


ridge = 0.5
exact = lax.Precision.HIGHEST


def from_partner(shard, axis, stride):
    return lax.ppermute(shard, axis, [(i, i ^ 1 << stride) for i in range(lax.axis_size(axis))])


def pair_scores(left_pts, right_pts):
    cross_term = jnp.einsum("...dn,...dm->...nm", left_pts, right_pts, precision=exact)
    left_sq = jnp.sum(left_pts * left_pts, axis=-2)
    right_sq = jnp.sum(right_pts * right_pts, axis=-2)
    dim_count = left_pts.shape[-2]
    return -(left_sq[..., :, None] + right_sq[..., None, :] - 2.0 * cross_term) / (2.0 * dim_count)


def interpolate(points, skeleton):
    return jax.nn.softmax(pair_scores(points, skeleton), axis=-1)


def kernel_block(left_pts, right_pts, leaf_size):
    return jnp.exp(pair_scores(left_pts, right_pts)) / leaf_size


def select_columns(blocks, index_list):
    return jnp.take_along_axis(blocks, index_list[:, None, :], axis=2)


def join_pairs(skeletons):
    node_count, dim_count, rank_size = skeletons.shape
    paired = skeletons.reshape(node_count // 2, 2, dim_count, rank_size).transpose(0, 2, 1, 3)
    return paired.reshape(node_count // 2, dim_count, 2 * rank_size)


def sibling_terms(values, couplings):
    first_half = jnp.einsum("ijb,iab->ija", values[1::2], couplings, precision=exact)
    second_half = jnp.einsum("ija,iab->ijb", values[0::2], couplings, precision=exact)
    return jnp.stack([first_half, second_half], axis=1).reshape(values.shape)


def column_sums(first_vec, second_vec):
    return jnp.sum(first_vec * second_vec, axis=1)


def per_device(coords, solution, residual, direction, order, leaf_skel, local_skel, upper_skel):
    leaves = leaf_skel.shape[0]
    dim_count, point_count = coords.shape
    leaf_size = point_count // leaves
    rhs_count = solution.shape[0]
    positions = jnp.arange(point_count, dtype=jnp.int32)
    inverse = jnp.zeros((point_count,), jnp.int32).at[order].set(positions)
    ordered = coords[:, order]
    leaf_points = ordered.reshape(dim_count, leaves, leaf_size).transpose(1, 0, 2)
    skeleton = select_columns(leaf_points, leaf_skel)
    leaf_kernel = lax.map(
        lambda block_pts: kernel_block(block_pts, block_pts, leaf_size), leaf_points
    )
    leaf_basis = interpolate(leaf_points, skeleton)
    local_transfers = []
    local_couplings = []
    width_now = leaves // 2
    while width_now >= 1:
        parent = select_columns(join_pairs(skeleton), local_skel)
        local_transfers.append(interpolate(skeleton, jnp.repeat(parent, 2, axis=0)))
        local_couplings.append(kernel_block(skeleton[0::2], skeleton[1::2], leaf_size))
        skeleton = parent
        width_now //= 2
    own_skel = skeleton[0]
    device_id = lax.axis_index("leaf")
    upper_steps = lax.axis_size("leaf").bit_length() - 1
    upper_transfers = []
    upper_couplings = []
    first_flags = []
    for step_index in range(upper_steps):
        other_skel = from_partner(own_skel, "leaf", step_index)
        is_first = device_id >> step_index & 1 == 0
        first_flags.append(is_first)
        upper_couplings.append(kernel_block(own_skel, other_skel, leaf_size))
        if step_index + 1 < upper_steps:
            joined = jnp.where(
                is_first,
                jnp.concatenate([own_skel, other_skel], axis=1),
                jnp.concatenate([other_skel, own_skel], axis=1),
            )
            parent_skel = jnp.take(joined, upper_skel[step_index, 0], axis=1)
            upper_transfers.append(interpolate(own_skel, parent_skel))
            own_skel = parent_skel
    iterate = solution[:, order]
    resid = residual[:, order]
    search = direction[:, order]
    norm_now = lax.psum(column_sums(resid, resid), "leaf")
    for step_index in range(ITERS):
        blocks = search.reshape(rhs_count, leaves, leaf_size)
        near_parts = jnp.einsum("jlq,lqp->ljp", blocks, leaf_kernel, precision=exact)
        coarse = jnp.einsum("jlq,lqr->ljr", blocks, leaf_basis, precision=exact)
        upward = [coarse]
        transfer = local_transfers[0]
        moved = jnp.einsum("cjr,crs->cjs", upward[-1], transfer, precision=exact)
        upward.append(moved[0::2] + moved[1::2])
        node_coef = upward[-1][0]
        coupled = []
        for apply_step_index in range(upper_steps):
            if apply_step_index + 1 < upper_steps:
                own_moved = jnp.dot(node_coef, upper_transfers[apply_step_index], precision=exact)
                other_coef, other_moved = from_partner(
                    (node_coef, own_moved), "leaf", apply_step_index
                )
                next_coef = jnp.where(
                    first_flags[apply_step_index], own_moved + other_moved, other_moved + own_moved
                )
            else:
                other_coef = from_partner(node_coef, "leaf", apply_step_index)
                next_coef = node_coef
            coupled.append(
                jnp.einsum(
                    "jb,ab->ja", other_coef, upper_couplings[apply_step_index], precision=exact
                )
            )
            node_coef = next_coef
        descent = coupled[upper_steps - 1]
        for apply_step_index in range(upper_steps - 2, -1, -1):
            descent = coupled[apply_step_index] + jnp.einsum(
                "js,rs->jr", descent, upper_transfers[apply_step_index], precision=exact
            )
        downward = descent[None]
        carried = jnp.einsum(
            "cjs,crs->cjr", jnp.repeat(downward, 2, axis=0), local_transfers[0], precision=exact
        )
        downward = sibling_terms(upward[0], local_couplings[0]) + carried
        far_parts = jnp.einsum("ljr,lqr->ljq", downward, leaf_basis, precision=exact)
        summed = near_parts + far_parts
        image = ridge * search + summed.transpose(1, 0, 2).reshape(rhs_count, point_count)
        curve_sum = lax.psum(column_sums(search, image), "leaf")
        step_size = norm_now / curve_sum
        iterate = iterate + step_size[:, None] * search
        resid = resid - step_size[:, None] * image
        norm_next = lax.psum(column_sums(resid, resid), "leaf")
        search = resid + (norm_next / norm_now)[:, None] * search
        norm_now = norm_next
    return (iterate[:, inverse], resid[:, inverse], search[:, inverse])


def solution(mesh):
    in_specs = (
        P(None, "leaf"),
        P(None, "leaf"),
        P(None, "leaf"),
        P(None, "leaf"),
        P("leaf"),
        P("leaf", None),
        P("leaf", None),
        P(None, "leaf", None),
    )
    out_specs = (P(None, "leaf"), P(None, "leaf"), P(None, "leaf"))
    return jax.shard_map(
        per_device, mesh=mesh, in_specs=in_specs, out_specs=out_specs, check_vma=False
    )
```

profile of v0, /device:TPU:1, one launch (start us, length us, event | category | flops | bytes accessed | tf_op | source)
XLA Modules:
  0.0 1194.5 jit_solution(6200594637827410153)
XLA Ops:
  3.3 2.9 copy.240
  6.3 12.4 %gather_fusion.3 = f32[4096,16]{1,0:T(8,128)S(1)} fusion(f32[16,4096]{0,1:T(8,128)} %copy.240, s32[4096]{0:T(1024)S(1)} %get-tuple-element.91), kind=kCustom, calls=%fused_computation.10 | custom fusion | bytes 540672 | tf_op jit(solution)/shard_map/gather | solution.py:60
  18.6 3.7 gather_fusion.8
  23.6 3.3 collective-permute-start.1
  29.6 15.8 %gather_fusion.2 = f32[4096,16]{1,0:T(8,128)} fusion(f32[16,4096]{0,1:T(8,128)} %copy.237, s32[4096]{0:T(1024)S(1)} %get-tuple-element.91), kind=kCustom, calls=%fused_computation.9 | custom fusion | bytes 540672 | tf_op jit(solution)/shard_map/gather | solution.py:98
  48.4 4.0 fusion.98
  55.7 3.5 fusion.37
  69.0 38.7 %while.10 = (s32[]{:T(128)}, f32[2,2048,2048]{2,1,0:T(8,128)}, f32[2,16,2048]{2,1,0:T(8,128)S(1)}, s32[]{:T(128)}) while((s32[]{:T(128)}, f32[2,2048,2048]{2,1,0:T(8,128)}, f32[2,16,2048]{2,1,0:T(8,128)S(1)}, s32[]{:T(128)}) %tuple.69), condition=%wide.region_4.5_spmd, body=%wide.region_2.4_spmd.sunk | while | flops 830535680 | bytes 17065024 | solution.py:63
  69.0 19.3 %bitcast_dynamic-update-slice_fusion.2 = f32[2,2048,2048]{2,1,0:T(8,128)} fusion(f32[2,2048,2048]{2,1,0:T(8,128)} %get-tuple-element.149, s32[]{:T(128)S(6)} %copy.332, f32[2048]{0:T(1024)S(1)} %fusion.428, f32[2,16,2048]{2,1,0:T(8,128)S(1)} %get-tuple-element.154), kind=kOutput, calls=%fused_computation.17.clone.1 | convolution fusion | flops 830472192 | bytes 16925696 | tf_op jit(solution)/shard_map/while/body/eval_jaxpr/...dn,...dm->...nm/dot_general | solution.py:18
  88.4 19.3 %bitcast_dynamic-update-slice_fusion.2 = f32[2,2048,2048]{2,1,0:T(8,128)} fusion(f32[2,2048,2048]{2,1,0:T(8,128)} %get-tuple-element.149, s32[]{:T(128)S(6)} %copy.332, f32[2048]{0:T(1024)S(1)} %fusion.428, f32[2,16,2048]{2,1,0:T(8,128)S(1)} %get-tuple-element.154), kind=kOutput, calls=%fused_computation.17.clone.1 | convolution fusion | flops 830472192 | bytes 16925696 | tf_op jit(solution)/shard_map/while/body/eval_jaxpr/...dn,...dm->...nm/dot_general | solution.py:18
  107.7 20.3 %fusion.39 = f32[2,16,2048]{2,1,0:T(8,128)} fusion(f32[2,2048,2048]{2,1,0:T(8,128)} %get-tuple-element.21, f32[2,2,8,2048]{3,2,1,0:T(8,128)S(1)} %bitcast.500), kind=kOutput, calls=%fused_computation.125 | convolution fusion | flops 1610612736 | bytes 34078720 | tf_op jit(solution)/shard_map/jlq,lqp->ljp/dot_general | solution.py:102
  131.1 15.8 %gather_fusion.1 = f32[4096,16]{1,0:T(8,128)} fusion(f32[16,4096]{0,1:T(8,128)} %copy.235, s32[4096]{0:T(1024)S(1)} %get-tuple-element.91), kind=kCustom, calls=%fused_computation.8 | custom fusion | bytes 540672 | tf_op jit(solution)/shard_map/gather | solution.py:97
  166.4 5.7 collective-permute-start.10
  218.2 3.6 collective-permute-start.9
  245.9 83.5 %all-reduce = (f32[16]{0:T(128)S(1)}, f32[16]{0:T(128)S(1)}) all-reduce(f32[16]{0:T(128)S(1)} %copy-done.80, f32[16]{0:T(128)S(1)} %get-tuple-element.117), channel_id=1, replica_groups=mesh['leaf'=256] {'leaf'}, use_global_device_ids=true, to_apply=%region_1.0 | all-reduce | flops 32 | bytes 256 | tf_op jit(solution)/shard_map/psum | solution.py:99
  331.4 72.7 %psum.65 = f32[16]{0:T(128)S(1)} all-reduce(f32[16]{0:T(128)S(1)} %get-tuple-element.70), channel_id=1, replica_groups=mesh['leaf'=256] {'leaf'}, use_global_device_ids=true, to_apply=%region_46.48 | all-reduce | flops 16 | bytes 128 | tf_op jit(solution)/shard_map/psum | solution.py:145
  405.7 5.7 fusion.123
  420.7 3.3 collective-permute-start.30
  424.0 3.4 collective-permute-done.30
  432.9 20.3 %fusion.122 = f32[2,16,2048]{2,1,0:T(8,128)} fusion(f32[16,2,2048]{2,0,1:T(8,128)S(1)} %fusion.43, f32[2,2048,2048]{2,1,0:T(8,128)} %get-tuple-element.21), kind=kOutput, calls=%fused_computation.331 | convolution fusion | flops 1610612736 | bytes 34078720 | tf_op jit(solution)/shard_map/jlq,lqp->ljp/dot_general | solution.py:102
  457.9 6.3 collective-permute-start.23
  484.6 77.4 %psum.66 = f32[16]{0:T(128)S(1)} all-reduce(f32[16]{0:T(128)S(1)} %get-tuple-element.119), channel_id=1, replica_groups=mesh['leaf'=256] {'leaf'}, use_global_device_ids=true, to_apply=%region_48.50 | all-reduce | flops 16 | bytes 128 | tf_op jit(solution)/shard_map/psum | solution.py:141
  564.6 73.1 %psum.67 = f32[16]{0:T(128)S(1)} all-reduce(f32[16]{0:T(128)S(1)} %get-tuple-element.68), channel_id=1, replica_groups=mesh['leaf'=256] {'leaf'}, use_global_device_ids=true, to_apply=%region_50.52 | all-reduce | flops 16 | bytes 128 | tf_op jit(solution)/shard_map/psum | solution.py:145
  640.0 5.7 fusion.141
  651.8 2.9 collective-permute-done.43
  654.9 3.6 collective-permute-start.45
  658.6 3.4 collective-permute-done.45
  667.4 19.6 %fusion.140 = f32[2,16,2048]{2,1,0:T(8,128)S(1)} fusion(f32[16,2,2048]{2,0,1:T(8,128)S(1)} %multiply_add_fusion.4, f32[2,2048,2048]{2,1,0:T(8,128)} %get-tuple-element.21), kind=kOutput, calls=%fused_computation.349 | convolution fusion | flops 1610612736 | bytes 34078720 | tf_op jit(solution)/shard_map/jlq,lqp->ljp/dot_general | solution.py:102
  691.7 6.5 collective-permute-start.38
  716.0 2.9 multiply_reduce_fusion.4
  718.9 77.6 %psum.68 = f32[16]{0:T(128)S(1)} all-reduce(f32[16]{0:T(128)S(1)} %get-tuple-element.121), channel_id=1, replica_groups=mesh['leaf'=256] {'leaf'}, use_global_device_ids=true, to_apply=%region_52.54 | all-reduce | flops 16 | bytes 128 | tf_op jit(solution)/shard_map/psum | solution.py:141
  799.1 72.7 %psum.69 = f32[16]{0:T(128)S(1)} all-reduce(f32[16]{0:T(128)S(1)} %get-tuple-element.66), channel_id=1, replica_groups=mesh['leaf'=256] {'leaf'}, use_global_device_ids=true, to_apply=%region_54.56 | all-reduce | flops 16 | bytes 128 | tf_op jit(solution)/shard_map/psum | solution.py:145
  873.9 5.7 fusion.159
  888.8 3.3 collective-permute-start.60
  892.2 16.2 %scatter_custom_fusion = s32[4096]{0:T(1024)} fusion(s32[4096]{0:T(1024)} %get-tuple-element.90, s32[4096]{0:T(1024)S(1)} %iota.3, s32[]{:T(128)} %constant.109.clone.1), kind=kCustom, calls=%fused_computation.272 | custom fusion | bytes 16896 | tf_op jit(solution)/shard_map/scatter | solution.py:59
  913.9 15.8 %gather_fusion = f32[4096,16]{1,0:T(8,128)} fusion(f32[16,4096]{0,1:T(8,128)} %copy.233, s32[4096]{0:T(1024)S(1)} %get-tuple-element.91), kind=kCustom, calls=%fused_computation.7 | custom fusion | bytes 540672 | tf_op jit(solution)/shard_map/gather | solution.py:96
  929.7 2.9 copy.234
  939.1 20.3 %fusion.158 = f32[2,16,2048]{2,1,0:T(8,128)} fusion(f32[16,2,2048]{2,0,1:T(8,128)S(1)} %multiply_add_fusion.2, f32[2,2048,2048]{2,1,0:T(8,128)} %get-tuple-element.21), kind=kOutput, calls=%fused_computation.367 | convolution fusion | flops 1610612736 | bytes 34078720 | tf_op jit(solution)/shard_map/jlq,lqp->ljp/dot_general | solution.py:102
  963.9 5.0 collective-permute-start.53
  970.5 3.2 collective-permute-start.59
  989.1 76.9 %psum.70 = f32[16]{0:T(128)S(1)} all-reduce(f32[16]{0:T(128)S(1)} %get-tuple-element.123), channel_id=1, replica_groups=mesh['leaf'=256] {'leaf'}, use_global_device_ids=true, to_apply=%region_56.58 | all-reduce | flops 16 | bytes 128 | tf_op jit(solution)/shard_map/psum | solution.py:141
  1066.3 73.2 %psum.71 = f32[16]{0:T(128)S(1)} all-reduce(f32[16]{0:T(128)S(1)} %multiply_reduce_fusion.1), channel_id=1, replica_groups=mesh['leaf'=256] {'leaf'}, use_global_device_ids=true, to_apply=%region_59.61 | all-reduce | flops 16 | bytes 128 | tf_op jit(solution)/shard_map/psum | solution.py:145
  1141.7 14.2 %gather_fusion.5 = f32[4096,16]{1,0:T(8,128)} fusion(f32[16,4096]{0,1:T(8,128)S(1)} %copy.277, s32[4096]{0:T(1024)S(1)} %fusion.76), kind=kCustom, calls=%fused_computation.12 | custom fusion | bytes 540672 | tf_op jit(solution)/shard_map/gather | solution.py:148
  1155.9 2.9 copy.281
  1159.4 14.2 %gather_fusion.6 = f32[4096,16]{1,0:T(8,128)} fusion(f32[16,4096]{0,1:T(8,128)S(1)} %copy.279, s32[4096]{0:T(1024)S(1)} %fusion.76), kind=kCustom, calls=%fused_computation.13 | custom fusion | bytes 540672 | tf_op jit(solution)/shard_map/gather | solution.py:148
  1173.6 2.9 copy.282
  1177.0 14.2 %gather_fusion.7 = f32[4096,16]{1,0:T(8,128)} fusion(f32[16,4096]{0,1:T(8,128)S(1)} %copy.280, s32[4096]{0:T(1024)S(1)} %fusion.76), kind=kCustom, calls=%fused_computation.14 | custom fusion | bytes 540672 | tf_op jit(solution)/shard_map/gather | solution.py:148
  1191.2 2.9 copy.283
  (570 shorter events, 247.7 us)
Async XLA Ops:
  23.6 126.8 %collective-permute-start.1 = (f32[16,256]{0,1:T(8,128)S(1)}, f32[16,256]{0,1:T(8,128)S(1)}, u32[]{:S(2)}, u32[]{:S(2)}) collective-permute-start(f32[16,256]{0,1:T(8,128)S(1)} %get-tuple-element.89), channel_id=1, source_target_pairs={{0,1},{1,0},{2,3},{3,2},{4,5},{5,4},{6,7},{7,6},{8,9},{9,8},{10,11... | collective-permute-start | bytes 49160 | tf_op jit(solution)/shard_map/ppermute | solution.py:14
  60.4 181.6 %collective-permute-start = (f32[16,256]{1,0:T(8,128)}, f32[16,256]{1,0:T(8,128)}, u32[]{:S(2)}, u32[]{:S(2)}) collective-permute-start(f32[16,256]{1,0:T(8,128)} %fusion.80), channel_id=1, source_target_pairs={{0,1},{1,0},{2,3},{3,2},{4,5},{5,4},{6,7},{7,6},{8,9},{9,8},{10,11... | collective-permute-start | bytes 49160 | tf_op jit(solution)/shard_map/ppermute | solution.py:14
  151.3 4.7 collective-permute-start.4
  153.2 7.0 collective-permute-start.2
  156.9 8.5 collective-permute-start.7
  160.8 79.8 %collective-permute-start.3 = (f32[16,256]{1,0:T(8,128)}, f32[16,256]{1,0:T(8,128)}, u32[]{:S(2)}, u32[]{:S(2)}) collective-permute-start(f32[16,256]{1,0:T(8,128)} %add.673), channel_id=1, source_target_pairs={{0,2},{1,3},{2,0},{3,1},{4,6},{5,7},{6,4},{7,5},{8,10},{9,11},{10,... | collective-permute-start | bytes 49160 | tf_op jit(solution)/shard_map/ppermute | solution.py:14
  162.3 10.6 collective-permute-start.5
  166.4 11.7 collective-permute-start.10
  173.5 65.7 %collective-permute-start.6 = (f32[16,256]{1,0:T(8,128)}, f32[16,256]{1,0:T(8,128)}, u32[]{:S(2)}, u32[]{:S(2)}) collective-permute-start(f32[16,256]{1,0:T(8,128)} %add.679), channel_id=1, source_target_pairs={{0,4},{1,5},{2,6},{3,7},{4,0},{5,1},{6,2},{7,3},{8,12},{9,13},{10,... | collective-permute-start | bytes 49160 | tf_op jit(solution)/shard_map/ppermute | solution.py:14
  175.1 6.6 collective-permute-start.8
  179.0 8.0 collective-permute-start.13
  183.3 9.5 collective-permute-start.11
  188.8 7.7 collective-permute-start.16
  194.4 7.6 collective-permute-start.14
  199.1 7.8 collective-permute-start.19
  203.6 10.9 collective-permute-start.17
  210.3 11.4 collective-permute-start.22
  218.2 19.5 %collective-permute-start.9 = (f32[16,256]{1,0:T(8,128)}, f32[16,256]{1,0:T(8,128)S(1)}, u32[]{:S(2)}, u32[]{:S(2)}) collective-permute-start(f32[16,256]{1,0:T(8,128)} %copy-done.52), channel_id=1, source_target_pairs={{0,8},{1,9},{2,10},{3,11},{4,12},{5,13},{6,14},{7,15},{8,0},{9,1},... | collective-permute-start | bytes 49160 | tf_op jit(solution)/shard_map/ppermute | solution.py:14
  221.8 4.2 collective-permute-start.21
  228.5 4.3 collective-permute-start.15
  416.9 3.6 collective-permute-start.28
  420.7 6.8 collective-permute-start.30
  431.5 21.7 %collective-permute-start.34 = (f32[16,256]{1,0:T(8,128)}, f32[16,256]{1,0:T(8,128)}, u32[]{:S(2)}, u32[]{:S(2)}) collective-permute-start(f32[16,256]{1,0:T(8,128)} %fusion.130), channel_id=1, source_target_pairs={{0,32},{1,33},{2,34},{3,35},{4,36},{5,37},{6,38},{7,39},{8,40},{9,... | collective-permute-start | bytes 49160 | tf_op jit(solution)/shard_map/ppermute | solution.py:14
  457.0 12.1 %collective-permute-start.37 = (f32[16,256]{1,0:T(8,128)S(1)}, f32[16,256]{1,0:T(8,128)S(1)}, u32[]{:S(2)}, u32[]{:S(2)}) collective-permute-start(f32[16,256]{1,0:T(8,128)S(1)} %add.733), channel_id=1, source_target_pairs={{0,128},{1,129},{2,130},{3,131},{4,132},{5,133},{6,134},{7,135},{8... | collective-permute-start | bytes 49160 | tf_op jit(solution)/shard_map/ppermute | solution.py:14
  457.9 23.7 %collective-permute-start.23 = (f32[16,256]{1,0:T(8,128)S(1)}, f32[16,256]{1,0:T(8,128)S(1)}, u32[]{:S(2)}, u32[]{:S(2)}) collective-permute-start(f32[16,256]{1,0:T(8,128)S(1)} %fusion.79), channel_id=1, source_target_pairs={{0,1},{1,0},{2,3},{3,2},{4,5},{5,4},{6,7},{7,6},{8,9},{9,8},{10,11... | collective-permute-start | bytes 49160 | tf_op jit(solution)/shard_map/ppermute | solution.py:14
  464.2 16.8 %collective-permute-start.25 = (f32[16,256]{1,0:T(8,128)S(1)}, f32[16,256]{1,0:T(8,128)S(1)}, u32[]{:S(2)}, u32[]{:S(2)}) collective-permute-start(f32[16,256]{1,0:T(8,128)S(1)} %add.727), channel_id=1, source_target_pairs={{0,2},{1,3},{2,0},{3,1},{4,6},{5,7},{6,4},{7,5},{8,10},{9,11},{10,... | collective-permute-start | bytes 49160 | tf_op jit(solution)/shard_map/ppermute | solution.py:14
  465.8 14.5 %collective-permute-start.27 = (f32[16,256]{1,0:T(8,128)S(1)}, f32[16,256]{1,0:T(8,128)S(1)}, u32[]{:S(2)}, u32[]{:S(2)}) collective-permute-start(f32[16,256]{1,0:T(8,128)S(1)} %add.728), channel_id=1, source_target_pairs={{0,4},{1,5},{2,6},{3,7},{4,0},{5,1},{6,2},{7,3},{8,12},{9,13},{10,... | collective-permute-start | bytes 49160 | tf_op jit(solution)/shard_map/ppermute | solution.py:14
  466.7 12.9 %collective-permute-start.29 = (f32[16,256]{1,0:T(8,128)S(1)}, f32[16,256]{1,0:T(8,128)S(1)}, u32[]{:S(2)}, u32[]{:S(2)}) collective-permute-start(f32[16,256]{1,0:T(8,128)S(1)} %add.729), channel_id=1, source_target_pairs={{0,8},{1,9},{2,10},{3,11},{4,12},{5,13},{6,14},{7,15},{8,0},{9,1},... | collective-permute-start | bytes 49160 | tf_op jit(solution)/shard_map/ppermute | solution.py:14
  471.7 4.3 collective-permute-start.33
  651.1 3.6 collective-permute-start.43
  654.9 7.0 collective-permute-start.45
  666.0 21.0 %collective-permute-start.49 = (f32[16,256]{1,0:T(8,128)}, f32[16,256]{1,0:T(8,128)}, u32[]{:S(2)}, u32[]{:S(2)}) collective-permute-start(f32[16,256]{1,0:T(8,128)} %fusion.148), channel_id=1, source_target_pairs={{0,32},{1,33},{2,34},{3,35},{4,36},{5,37},{6,38},{7,39},{8,40},{9,... | collective-permute-start | bytes 49160 | tf_op jit(solution)/shard_map/ppermute | solution.py:14
  690.8 12.0 %collective-permute-start.52 = (f32[16,256]{1,0:T(8,128)S(1)}, f32[16,256]{1,0:T(8,128)S(1)}, u32[]{:S(2)}, u32[]{:S(2)}) collective-permute-start(f32[16,256]{1,0:T(8,128)S(1)} %add.756), channel_id=1, source_target_pairs={{0,128},{1,129},{2,130},{3,131},{4,132},{5,133},{6,134},{7,135},{8... | collective-permute-start | bytes 49160 | tf_op jit(solution)/shard_map/ppermute | solution.py:14
  691.7 23.6 %collective-permute-start.38 = (f32[16,256]{1,0:T(8,128)S(1)}, f32[16,256]{1,0:T(8,128)S(1)}, u32[]{:S(2)}, u32[]{:S(2)}) collective-permute-start(f32[16,256]{1,0:T(8,128)S(1)} %fusion.78), channel_id=1, source_target_pairs={{0,1},{1,0},{2,3},{3,2},{4,5},{5,4},{6,7},{7,6},{8,9},{9,8},{10,11... | collective-permute-start | bytes 49160 | tf_op jit(solution)/shard_map/ppermute | solution.py:14
  698.2 16.4 %collective-permute-start.40 = (f32[16,256]{1,0:T(8,128)S(1)}, f32[16,256]{1,0:T(8,128)S(1)}, u32[]{:S(2)}, u32[]{:S(2)}) collective-permute-start(f32[16,256]{1,0:T(8,128)S(1)} %add.750), channel_id=1, source_target_pairs={{0,2},{1,3},{2,0},{3,1},{4,6},{5,7},{6,4},{7,5},{8,10},{9,11},{10,... | collective-permute-start | bytes 49160 | tf_op jit(solution)/shard_map/ppermute | solution.py:14
  699.3 14.7 %collective-permute-start.42 = (f32[16,256]{1,0:T(8,128)S(1)}, f32[16,256]{1,0:T(8,128)S(1)}, u32[]{:S(2)}, u32[]{:S(2)}) collective-permute-start(f32[16,256]{1,0:T(8,128)S(1)} %add.751), channel_id=1, source_target_pairs={{0,4},{1,5},{2,6},{3,7},{4,0},{5,1},{6,2},{7,3},{8,12},{9,13},{10,... | collective-permute-start | bytes 49160 | tf_op jit(solution)/shard_map/ppermute | solution.py:14
  700.2 13.1 %collective-permute-start.44 = (f32[16,256]{1,0:T(8,128)S(1)}, f32[16,256]{1,0:T(8,128)S(1)}, u32[]{:S(2)}, u32[]{:S(2)}) collective-permute-start(f32[16,256]{1,0:T(8,128)S(1)} %add.752), channel_id=1, source_target_pairs={{0,8},{1,9},{2,10},{3,11},{4,12},{5,13},{6,14},{7,15},{8,0},{9,1},... | collective-permute-start | bytes 49160 | tf_op jit(solution)/shard_map/ppermute | solution.py:14
  705.4 4.3 collective-permute-start.48
  885.1 3.6 collective-permute-start.58
  888.8 19.6 %collective-permute-start.60 = (f32[16,256]{1,0:T(8,128)S(1)}, f32[16,256]{1,0:T(8,128)}, u32[]{:S(2)}, u32[]{:S(2)}) collective-permute-start(f32[16,256]{1,0:T(8,128)S(1)} %fusion.164), channel_id=1, source_target_pairs={{0,8},{1,9},{2,10},{3,11},{4,12},{5,13},{6,14},{7,15},{8,0},{9,1},... | collective-permute-start | bytes 49160 | tf_op jit(solution)/shard_map/ppermute | solution.py:14
  910.0 25.0 %collective-permute-start.62 = (f32[16,256]{1,0:T(8,128)}, f32[16,256]{1,0:T(8,128)}, u32[]{:S(2)}, u32[]{:S(2)}) collective-permute-start(f32[16,256]{1,0:T(8,128)} %fusion.165), channel_id=1, source_target_pairs={{0,16},{1,17},{2,18},{3,19},{4,20},{5,21},{6,22},{7,23},{8,24},{9,... | collective-permute-start | bytes 49160 | tf_op jit(solution)/shard_map/ppermute | solution.py:14
  936.6 22.8 %collective-permute-start.64 = (f32[16,256]{1,0:T(8,128)}, f32[16,256]{1,0:T(8,128)}, u32[]{:S(2)}, u32[]{:S(2)}) collective-permute-start(f32[16,256]{1,0:T(8,128)} %fusion.166), channel_id=1, source_target_pairs={{0,32},{1,33},{2,34},{3,35},{4,36},{5,37},{6,38},{7,39},{8,40},{9,... | collective-permute-start | bytes 49160 | tf_op jit(solution)/shard_map/ppermute | solution.py:14
  963.1 10.5 collective-permute-start.67
  963.9 22.3 %collective-permute-start.53 = (f32[16,256]{1,0:T(8,128)S(1)}, f32[16,256]{1,0:T(8,128)S(1)}, u32[]{:S(2)}, u32[]{:S(2)}) collective-permute-start(f32[16,256]{1,0:T(8,128)S(1)} %fusion.77), channel_id=1, source_target_pairs={{0,1},{1,0},{2,3},{3,2},{4,5},{5,4},{6,7},{7,6},{8,9},{9,8},{10,11... | collective-permute-start | bytes 49160 | tf_op jit(solution)/shard_map/ppermute | solution.py:14
  968.9 16.7 %collective-permute-start.55 = (f32[16,256]{1,0:T(8,128)S(1)}, f32[16,256]{1,0:T(8,128)S(1)}, u32[]{:S(2)}, u32[]{:S(2)}) collective-permute-start(f32[16,256]{1,0:T(8,128)S(1)} %add.773), channel_id=1, source_target_pairs={{0,2},{1,3},{2,0},{3,1},{4,6},{5,7},{6,4},{7,5},{8,10},{9,11},{10,... | collective-permute-start | bytes 49160 | tf_op jit(solution)/shard_map/ppermute | solution.py:14
  970.4 14.4 %collective-permute-start.57 = (f32[16,256]{1,0:T(8,128)S(1)}, f32[16,256]{1,0:T(8,128)S(1)}, u32[]{:S(2)}, u32[]{:S(2)}) collective-permute-start(f32[16,256]{1,0:T(8,128)S(1)} %add.774), channel_id=1, source_target_pairs={{0,4},{1,5},{2,6},{3,7},{4,0},{5,1},{6,2},{7,3},{8,12},{9,13},{10,... | collective-permute-start | bytes 49160 | tf_op jit(solution)/shard_map/ppermute | solution.py:14
  970.5 13.6 %collective-permute-start.59 = (f32[16,256]{1,0:T(8,128)S(1)}, f32[16,256]{1,0:T(8,128)S(1)}, u32[]{:S(2)}, u32[]{:S(2)}) collective-permute-start(f32[16,256]{1,0:T(8,128)S(1)} %add.775), channel_id=1, source_target_pairs={{0,8},{1,9},{2,10},{3,11},{4,12},{5,13},{6,14},{7,15},{8,0},{9,1},... | collective-permute-start | bytes 49160 | tf_op jit(solution)/shard_map/ppermute | solution.py:14
  976.5 4.3 collective-permute-start.63
  (105 other events, 4254.2 us)
where the time goes:
time: 1210 us; the launch traced here: 1190 us
  blocking collectives  607 us (50%)
  matrix products  213 us (18%)
  local copies, waits for them, and re-layouts  166 us (14%)
  starting transfers between devices  107 us (9%)
  waiting for transfers between devices  57.3 us (5%)
  other arithmetic  40.9 us (3%)
    psum x4, blocking collectives, per_device(): norm_next = lax.psum(column_sums(resid, resid), 'leaf')  292 us
    psum x3, blocking collectives, per_device(): curve_sum = lax.psum(column_sums(search, image), 'leaf')  232 us
    ppermute x68, starting transfers between devices, from_partner(): lax.ppermute(shard, axis, [(i, i ^ 1 << stride) for i in range(lax.axis_s...  107 us
    psum x1, blocking collectives, per_device(): norm_now = lax.psum(column_sums(resid, resid), 'leaf')  83.5 us
    dot_general x4, matrix products, per_device(): jnp.einsum('jlq,lqp->ljp', blocks, leaf_kernel, precision=exact)  80.4 us
    dot_general x20, matrix products, pair_scores(): jnp.einsum('...dn,...dm->...nm', left_pts, right_pts, precision=exact)  59.5 us
    ppermute x68, waiting for transfers between devices, from_partner(): lax.ppermute(shard, axis, [(i, i ^ 1 << stride) for i in range(lax.axis_s...  57.3 us
    gather x3, local copies, waits for them, and re-layouts, per_device(): return (iterate[:, inverse], resid[:, inverse], search[:, inverse])  42.6 us
  transfers between devices with their start and end apart: 68, of which 46 were waited for; matrix products, arithmetic and copies ran while one was open for 24% of the time, Pallas kernels for 0%

commit v1 on v0

v1 whole, which is shorter than its diff:
```python
import math

import jax
import jax.numpy as jnp
from jax import lax
from jax.experimental import pallas as pl
from jax.experimental.pallas import tpu as pltpu
from jax.sharding import PartitionSpec as P

ITERS = 4
MESH = pl.DeviceIdType.MESH
LANES = 128
LOG2E = math.log2(math.e)
F32 = jnp.float32
BF16 = jnp.bfloat16
VMEM = pl.BlockSpec(memory_space=pltpu.VMEM)

OWN0, OWN1, OWN2, OWN3, UP0, UP1, SIB, COUSIN, UNCLE, DOWN0, DOWN1 = range(11)
PER_ROUND = 11


def pick(sources, index_row, first_block, block_count):
    low = index_row & (LANES - 1)
    high = index_row >> 7
    outs = [None] * len(sources)
    for block in range(block_count):
        hit = None
        for n, source in enumerate(sources):
            held = source(first_block + block)
            rows = held.shape[0]
            place = jnp.broadcast_to(low, (rows, LANES))
            got = jnp.take_along_axis(held, place, axis=1, mode="promise_in_bounds")
            if outs[n] is None:
                outs[n] = got
            else:
                hit = jnp.broadcast_to(high, (rows, LANES)) == block
                outs[n] = jnp.where(hit, got, outs[n])
    return outs


def block_of(ref):
    return lambda b: ref[:, b * LANES : (b + 1) * LANES]


def arrange(coords, resid, search, order, leaf_skel, local_skel, pts, r_out, p_out, inverse, skel, parent, digits, marks):
    blocks = order.shape[0]
    sources = [block_of(coords), block_of(resid), block_of(search)]

    def body(ob, carry):
        row = order[pl.ds(ob, 1), :]
        got = pick(sources, row, 0, blocks)
        span = pl.ds(pl.multiple_of(ob * LANES, LANES), LANES)
        for ref, value in zip((pts, r_out, p_out), got):
            ref[:, span] = value
        place = ob * LANES + lax.broadcasted_iota(jnp.int32, (blocks, LANES), 1)
        hit = lax.broadcasted_iota(jnp.int32, (blocks, LANES), 0) == (row >> 7)
        coarse = jnp.where(hit, (place >> 5).astype(F32), 0.0)
        fine = jnp.where(hit, (place & 31).astype(F32), 0.0)
        digits[0:blocks, span] = coarse.astype(BF16)
        digits[blocks : 2 * blocks, span] = fine.astype(BF16)
        lane_hit = lax.broadcasted_iota(jnp.int32, (LANES, LANES), 0) == (row & (LANES - 1))
        marks[:, span] = jnp.where(lane_hit, 1.0, 0.0).astype(BF16)
        return carry

    lax.fori_loop(0, blocks, body, 0)
    found = lax.dot_general(digits[...], marks[...], (((1,), (1,)), ((), ())), preferred_element_type=F32)
    inverse[...] = (found[0:blocks] * 32.0 + found[blocks : 2 * blocks]).astype(jnp.int32)
    leaves = skel.shape[0]
    rank = leaf_skel.shape[1]
    leaf_blocks = blocks // leaves
    for leaf in range(leaves):
        for ob in range(rank // LANES):
            row = leaf_skel[leaf : leaf + 1, ob * LANES : (ob + 1) * LANES]
            (got,) = pick([block_of(pts)], row, leaf * leaf_blocks, leaf_blocks)
            skel[leaf, :, ob * LANES : (ob + 1) * LANES] = got
    per = rank // LANES
    both = lambda b: skel[b // per, :, (b % per) * LANES : (b % per + 1) * LANES]
    for ob in range(per):
        row = local_skel[0:1, ob * LANES : (ob + 1) * LANES]
        (got,) = pick([both], row, 0, 2 * per)
        parent[:, ob * LANES : (ob + 1) * LANES] = got


def restore(x_in, gain, resid, search, inverse, x_out, r_out, p_out):
    blocks = inverse.shape[0]
    sources = [block_of(gain), block_of(resid), block_of(search)]

    def body(ob, carry):
        row = inverse[pl.ds(ob, 1), :]
        span = pl.ds(pl.multiple_of(ob * LANES, LANES), LANES)
        got = pick(sources, row, 0, blocks)
        x_out[:, span] = x_in[:, span] + got[0]
        r_out[:, span] = got[1]
        p_out[:, span] = got[2]
        return carry

    lax.fori_loop(0, blocks, body, 0)


def split(value):
    high = value.astype(BF16)
    return high, (value - high.astype(F32)).astype(BF16)


def split3(value):
    high = value.astype(BF16)
    rest = value - high.astype(F32)
    mid = rest.astype(BF16)
    return high, mid, (rest - mid.astype(F32)).astype(BF16)


def mm(a, b):
    return jnp.dot(a, b, preferred_element_type=F32)


def norm_rows(norms, first):
    high, mid, low = (part.astype(F32) for part in split3(norms))
    shape = (16, norms.shape[1])
    row = lax.broadcasted_iota(jnp.int32, shape, 0)
    one = jnp.where((row >= 3 - first) & (row < 6 - first), 1.0, 0.0)
    tile = jnp.where(row == first, high, one)
    tile = jnp.where(row == first + 1, mid, tile)
    return jnp.where(row == first + 2, low, tile)


def left_form(points):
    high, mid, low = (part.astype(F32) for part in split3(points))
    norms = jnp.sum(points * points, axis=0, keepdims=True) * (-LOG2E / 32.0)
    extra = norm_rows(norms, 0)
    full = jnp.concatenate([high, high, mid, mid, high, low, extra, jnp.zeros_like(extra)], axis=0)
    return jnp.transpose(full, (1, 0)).astype(BF16)


def right_form(points):
    high, mid, low = split3(points * (LOG2E / 16.0))
    norms = jnp.sum(points * points, axis=0, keepdims=True) * (-LOG2E / 32.0)
    extra = norm_rows(norms, 3).astype(BF16)
    return jnp.concatenate([high, mid, high, mid, low, high, extra, jnp.zeros_like(extra)], axis=0)


def softmax2(scores, axis):
    weights = jnp.exp2(scores - jnp.max(scores, axis=axis, keepdims=True))
    return weights / jnp.sum(weights, axis=axis, keepdims=True)


def row_dot(a, b):
    return jnp.sum(a * b, axis=1, keepdims=True)


def solve(pts, r_in, p_in, skel0, skel1, upper, gain, r_out, p_out,
          near_mat, uq_hi, uq_lo, ut_hi, ut_lo, t_hi, t_lo, vec, vsplit, image, q_ref,
          state, points_out, points_in, coef_out, coef_in, sum_out, sum_in, cps,
          send_sem, recv_sem):
    me = lax.axis_index("leaf")
    rounds = 4
    leaf_size = near_mat.shape[1]
    leaves = near_mat.shape[0]
    scale = 1.0 / leaf_size
    rank = skel1.shape[1]
    local = rounds * PER_ROUND
    bits = [(me // (1 << u)) % 2 for u in range(2 * rounds)]

    def partner(g, t):
        step = 1 << (2 * g)
        low = (1 - 2 * bits[2 * g]) * step
        high = (1 - 2 * bits[2 * g + 1]) * (2 * step)
        return me + (t % 2) * low + (t // 2) * high

    barrier = pltpu.get_barrier_semaphore()
    for g in range(rounds):
        for t in range(1, 4):
            pl.semaphore_signal(barrier, inc=1, device_id=(partner(g, t),), device_id_type=MESH)
    pl.semaphore_wait(barrier, 3 * rounds)

    def copies(src, dst, phase, g):
        return [
            pltpu.make_async_remote_copy(
                src_ref=src,
                dst_ref=dst.at[t - 1],
                send_sem=send_sem.at[g, t - 1],
                recv_sem=recv_sem.at[phase, g, t - 1],
                device_id=(partner(g, t),),
                device_id_type=MESH,
            )
            for t in range(1, 4)
        ]

    def keep(slot, value):
        high, low = split(value)
        t_hi[slot] = high
        t_lo[slot] = low

    def times(value, slot):
        high, low = split(value)
        rows = value.shape[0]
        wide = mm(jnp.concatenate([high, low], axis=0), t_hi[slot])
        return wide[:rows] + wide[rows:] + mm(high, t_lo[slot])

    def choose(first_is_own, index_row, own, other):
        swapped = jnp.where(index_row >= rank, index_row - rank, index_row + rank)
        want = jnp.where(first_is_own, index_row, swapped)
        place = lax.broadcasted_iota(jnp.int32, (rank, rank), 0).astype(F32)
        got = None
        for n, points in enumerate((own, other)):
            hot = jnp.where(place + float(n * rank) == want, 1.0, 0.0).astype(BF16)
            wide = mm(jnp.concatenate(split3(points), axis=0), hot)
            part = (wide[0:16] + wide[16:32]) + wide[32:48]
            got = part if got is None else got + part
        return got

    rows_part = leaf_size // 8

    def near_rows(part):
        leaf = part // 2
        right = right_form(pts[:, leaf * leaf_size : (leaf + 1) * leaf_size])

        def body(j, carry):
            span = pl.ds(pl.multiple_of(((part % 2) * 4 + j) * rows_part, rows_part), rows_part)
            near_mat[leaf, span, :] = jnp.exp2(mm(lefts[leaf, span, :], right)).astype(BF16)
            return carry

        lax.fori_loop(0, 4, body, 0)

    lefts = uq_hi.at[:, :, 0:LANES]
    own = skel1[...]
    for g in range(rounds):
        u = 2 * g
        points_out[g, 0:16, :] = own
        points_out[g, 16:24, :] = jnp.broadcast_to(upper[u : u + 1, :].astype(F32), (8, rank))
        sends = copies(points_out.at[g], points_in.at[g], 0, g)
        for c in sends:
            c.start()
        if g == 0:
            for leaf in range(leaves):
                lefts[leaf] = left_form(pts[:, leaf * leaf_size : (leaf + 1) * leaf_size])
        near_rows(g)
        for c in sends:
            c.wait()
        low = [own] + [points_in[g, t, 0:16, :] for t in range(3)]
        lists = [points_out[g, 16:17, :], points_in[g, 1, 16:17, :]]
        mids = [choose(bits[u] == 0, lists[n], low[2 * n], low[2 * n + 1]) for n in range(2)]
        low_left = [left_form(x) for x in low]
        mid_left = [left_form(x) for x in mids]
        low_right = [right_form(low[0]), None, right_form(low[2])]
        mid_right = [right_form(x) for x in mids]
        base = g * PER_ROUND
        for t in range(4):
            keep(base + OWN0 + t, softmax2(mm(low_left[t], mid_right[t // 2]), 1))
        keep(base + DOWN0, softmax2(mm(mid_left[0], low_right[0]), 0))
        keep(base + SIB, jnp.exp2(mm(low_left[1], low_right[0])) * scale)
        keep(base + COUSIN, jnp.exp2(mm(low_left[3], low_right[2])) * scale)
        keep(base + UNCLE, jnp.exp2(mm(mid_left[1], mid_right[0])) * scale)
        if g + 1 < rounds:
            top = choose(bits[u + 1] == 0, upper[u + 1 : u + 2, :].astype(F32), mids[0], mids[1])
            top_right = right_form(top)
            for n in range(2):
                keep(base + UP0 + n, softmax2(mm(mid_left[n], top_right), 1))
            keep(base + DOWN1, softmax2(mm(left_form(top), mid_right[0]), 0))
            own = top

    skel_left = [left_form(skel0[leaf]) for leaf in range(leaves)]
    skel_right = [right_form(skel0[leaf]) for leaf in range(leaves)]
    parent_left = left_form(skel1[...])
    parent_right = right_form(skel1[...])
    for leaf in range(leaves):
        keep(local + leaf, softmax2(mm(skel_left[leaf], parent_right), 1))
        keep(local + 2 + leaf, softmax2(mm(parent_left, skel_right[leaf]), 0))
        keep(local + 4 + leaf, jnp.exp2(mm(skel_left[1 - leaf], skel_right[leaf])) * scale)

    for leaf in range(leaves):

        def basis_rows(j, carry, leaf=leaf):
            span = pl.ds(pl.multiple_of(j * rank, rank), rank)
            high, low = split(softmax2(mm(lefts[leaf, span, :], skel_right[leaf]), 1))
            uq_lo[leaf, span, :] = low
            uq_hi[leaf, span, :] = high
            return carry

        lax.fori_loop(0, leaf_size // rank, basis_rows, 0)
        right = right_form(pts[:, leaf * leaf_size : (leaf + 1) * leaf_size])
        high, low = split(softmax2(mm(skel_left[leaf], right), 0))
        ut_hi[leaf] = high
        ut_lo[leaf] = low

    vec[...] = p_in[...]
    r_out[...] = r_in[...]
    p_out[...] = jnp.zeros_like(p_out)
    q_ref[...] = jnp.zeros_like(q_ref)
    gain[...] = jnp.zeros_like(gain)
    state[0] = jnp.ones(state.shape[1:], F32)
    state[1] = jnp.zeros(state.shape[1:], F32)
    rhs = vec.shape[0]
    lane = lax.broadcasted_iota(jnp.int32, (rhs, LANES), 1)

    def iteration(k, carry):
        high, low = split(vec[...])
        vsplit[0:rhs, :] = high
        vsplit[rhs : 2 * rhs, :] = low
        fresh = row_dot(r_out[...], r_out[...])
        cross = row_dot(r_out[...], q_ref[...])
        for leaf in range(leaves):

            def near_columns(j, carry, leaf=leaf):
                inner = pl.ds(pl.multiple_of(j * rank, rank), rank)
                span = pl.ds(pl.multiple_of(leaf * leaf_size + j * rank, rank), rank)
                wide = mm(vsplit[:, leaf * leaf_size : (leaf + 1) * leaf_size], near_mat[leaf, :, inner])
                image[:, span] = 0.5 * vec[:, span] + (wide[:rhs] + wide[rhs:]) * scale
                return carry

            lax.fori_loop(0, leaf_size // rank, near_columns, 0)
        total = row_dot(vec[...], image[...])
        leaf_coef = []
        for leaf in range(leaves):
            cols = slice(leaf * leaf_size, (leaf + 1) * leaf_size)
            wide = mm(vsplit[:, cols], uq_hi[leaf])
            leaf_coef.append(wide[:rhs] + wide[rhs:] + mm(vsplit[0:rhs, cols], uq_lo[leaf]))
        coef = times(leaf_coef[0], local) + times(leaf_coef[1], local + 1)
        leaf_cp = [times(leaf_coef[1 - leaf], local + 4 + leaf) for leaf in range(leaves)]
        total = total + 2.0 * row_dot(leaf_coef[0], leaf_cp[0])
        sums = jnp.where(lane == 0, fresh, 0.0)
        sums = jnp.where(lane == 1, cross, sums)
        sums = jnp.where(lane == 2, total, sums)
        for g in range(rounds):
            base = g * PER_ROUND
            coef_out[g, :, 0:rank] = coef
            coef_out[g, :, rank : rank + LANES] = sums
            sends = copies(coef_out.at[g], coef_in.at[k, g], 1 + k, g)
            for c in sends:
                c.start()
            for c in sends:
                c.wait()
            got = [coef] + [coef_in[k, g, t, :, 0:rank] for t in range(3)]
            far = [coef_in[k, g, t, :, rank : rank + LANES] for t in range(3)]
            mid0 = times(got[0], base + OWN0) + times(got[1], base + OWN1)
            mid1 = times(got[2], base + OWN2) + times(got[3], base + OWN3)
            if g + 1 < rounds:
                coef = times(mid0, base + UP0) + times(mid1, base + UP1)
            low_cp = times(got[1], base + SIB)
            mid_cp = times(mid1, base + UNCLE)
            cps[2 * g] = low_cp
            cps[2 * g + 1] = mid_cp
            quad = row_dot(got[0], low_cp) + row_dot(got[2], times(got[3], base + COUSIN)) + row_dot(mid0, mid_cp)
            sums = (sums + far[0]) + (far[1] + far[2]) + jnp.where(lane == 2, 2.0 * quad, 0.0)
        down = cps[2 * rounds - 1]
        for u in range(2 * rounds - 2, -1, -1):
            down = cps[u] + times(down, (u // 2) * PER_ROUND + (DOWN1 if u % 2 else DOWN0))
        for leaf in range(leaves):
            cols = slice(leaf * leaf_size, (leaf + 1) * leaf_size)
            leaf_down = leaf_cp[leaf] + times(down, local + 2 + leaf)
            high, low = split(leaf_down)
            wide = mm(jnp.concatenate([high, low], axis=0), ut_hi[leaf])
            image[:, cols] += wide[:rhs] + wide[rhs:] + mm(high, ut_lo[leaf])
        fresh = sums[:, 0:1]
        cross = sums[:, 1:2]
        beta = fresh / state[0, :, 0:1]
        curve = sums[:, 2:3] + 2.0 * beta * cross + beta * beta * state[1, :, 0:1]
        alpha = fresh / curve
        state[0] = jnp.broadcast_to(fresh, (rhs, LANES))
        state[1] = jnp.broadcast_to(curve, (rhs, LANES))
        p_new = vec[...] + beta * p_out[...]
        q_new = image[...] + beta * q_ref[...]
        p_out[...] = p_new
        q_ref[...] = q_new
        gain[...] += alpha * p_new
        r_new = r_out[...] - alpha * q_new
        r_out[...] = r_new
        vec[...] = r_new
        return carry

    lax.fori_loop(0, ITERS, iteration, 0)
    sums = jnp.broadcast_to(row_dot(r_out[...], r_out[...]), (rhs, LANES))
    for g in range(rounds):
        sum_out[g] = sums
        sends = copies(sum_out.at[g], sum_in.at[g], 1 + ITERS, g)
        for c in sends:
            c.start()
        for c in sends:
            c.wait()
        sums = (sums + sum_in[g, 0]) + (sum_in[g, 1] + sum_in[g, 2])
    beta = sums[:, 0:1] / state[0, :, 0:1]
    p_out[...] = r_out[...] + beta * p_out[...]


def per_device(coords, solution, residual, direction, order, leaf_skel, local_skel, upper_skel):
    dims, count = coords.shape
    rhs = solution.shape[0]
    leaves, rank = leaf_skel.shape
    leaf_size = count // leaves
    blocks = count // LANES
    flat = jax.ShapeDtypeStruct((rhs, count), F32)
    limit = 60 * 1024 * 1024
    pts, resid, search, inverse, skel0, skel1 = pl.pallas_call(
        arrange,
        out_shape=(
            jax.ShapeDtypeStruct((dims, count), F32),
            flat,
            flat,
            jax.ShapeDtypeStruct((blocks, LANES), jnp.int32),
            jax.ShapeDtypeStruct((leaves, dims, rank), F32),
            jax.ShapeDtypeStruct((dims, rank), F32),
        ),
        in_specs=[VMEM] * 6,
        out_specs=(VMEM,) * 6,
        scratch_shapes=[pltpu.VMEM((2 * blocks, count), BF16), pltpu.VMEM((LANES, count), BF16)],
        compiler_params=pltpu.CompilerParams(vmem_limit_bytes=limit),
    )(coords, residual, direction, order.reshape(blocks, LANES), leaf_skel, local_skel)
    slots = 4 * PER_ROUND + 6
    gain, resid, search = pl.pallas_call(
        solve,
        out_shape=(flat, flat, flat),
        in_specs=[VMEM] * 6,
        out_specs=(VMEM,) * 3,
        scratch_shapes=[
            pltpu.VMEM((leaves, leaf_size, leaf_size), BF16),
            pltpu.VMEM((leaves, leaf_size, rank), BF16),
            pltpu.VMEM((leaves, leaf_size, rank), BF16),
            pltpu.VMEM((leaves, rank, leaf_size), BF16),
            pltpu.VMEM((leaves, rank, leaf_size), BF16),
            pltpu.VMEM((slots, rank, rank), BF16),
            pltpu.VMEM((slots, rank, rank), BF16),
            pltpu.VMEM((rhs, count), F32),
            pltpu.VMEM((2 * rhs, count), BF16),
            pltpu.VMEM((rhs, count), F32),
            pltpu.VMEM((rhs, count), F32),
            pltpu.VMEM((2, rhs, LANES), F32),
            pltpu.VMEM((4, dims + 8, rank), F32),
            pltpu.VMEM((4, 3, dims + 8, rank), F32),
            pltpu.VMEM((4, rhs, rank + LANES), F32),
            pltpu.VMEM((ITERS, 4, 3, rhs, rank + LANES), F32),
            pltpu.VMEM((4, rhs, LANES), F32),
            pltpu.VMEM((4, 3, rhs, LANES), F32),
            pltpu.VMEM((8, rhs, rank), F32),
            pltpu.SemaphoreType.DMA((4, 3)),
            pltpu.SemaphoreType.DMA((ITERS + 2, 4, 3)),
        ],
        compiler_params=pltpu.CompilerParams(vmem_limit_bytes=limit, collective_id=0, has_side_effects=True),
    )(pts, resid, search, skel0, skel1, upper_skel.reshape(-1, rank))
    return pl.pallas_call(
        restore,
        out_shape=(flat, flat, flat),
        in_specs=[VMEM] * 5,
        out_specs=(VMEM,) * 3,
        compiler_params=pltpu.CompilerParams(vmem_limit_bytes=limit),
    )(solution, gain, resid, search, inverse)


def solution(mesh):
    in_specs = (
        P(None, "leaf"),
        P(None, "leaf"),
        P(None, "leaf"),
        P(None, "leaf"),
        P("leaf"),
        P("leaf", None),
        P("leaf", None),
        P(None, "leaf", None),
    )
    out_specs = (P(None, "leaf"), P(None, "leaf"), P(None, "leaf"))
    return jax.shard_map(
        per_device, mesh=mesh, in_specs=in_specs, out_specs=out_specs, check_vma=False
    )
```

time: 1210 us -> 185 us (0.15); the launches traced: 1190 us -> 184 us
  blocking collectives: 607 us -> 0 us
  matrix products: 213 us -> 0 us
  Pallas kernels: 0 us -> 182 us
  local copies, waits for them, and re-layouts: 166 us -> 1.29 us
  starting transfers between devices: 107 us -> 0 us
  waiting for transfers between devices: 57.3 us -> 0 us
  other arithmetic: 40.9 us -> 0 us
    psum x8 -> x0, blocking collectives: 607 us -> none  [the longest x4 292 us: per_device(): norm_next = lax.psum(column_sums(resid, resid), 'leaf')]
    dot_general x136 -> x0, matrix products: 213 us -> none  [the longest x4 80.4 us: per_device(): jnp.einsum('jlq,lqp->ljp', blocks, leaf_kernel, precision=exact)]
    pallas_call x0 -> x3, Pallas kernels: none -> 182 us  [the longest x1 160 us: per_device(): pl.pallas_call(solve, out_shape=(flat, flat, flat), in_specs=[VMEM] * 6,...]
    gather x20 -> x0, local copies, waits for them, and re-layouts: 121 us -> none  [the longest x3 42.6 us: per_device(): return (iterate[:, inverse], resid[:, inverse], search[:, inverse])]
    ppermute x68 -> x0, starting transfers between devices: 107 us -> none  [from_partner(): lax.ppermute(shard, axis, [(i, i ^ 1 << stride) for i in range(lax.axis_s...]
    ppermute x68 -> x0, waiting for transfers between devices: 57.3 us -> none  [from_partner(): lax.ppermute(shard, axis, [(i, i ^ 1 << stride) for i in range(lax.axis_s...]
    unnamed x178 -> x1, local copies, waits for them, and re-layouts: 23.2 us -> 1.29 us
    scatter x1 -> x0, local copies, waits for them, and re-layouts: 16.2 us -> none  [per_device(): inverse = jnp.zeros((point_count,), jnp.int32).at[order].set(positions)]
  transfers between devices with their start and end apart: 68 -> 0, of which waited for: 46 -> 0; matrix products, arithmetic and copies ran while one was open for 24% -> 0% of each run, Pallas kernels for 0% -> 0%
where the time goes in v1:
time: 185 us; the launch traced here: 184 us
  Pallas kernels  182 us (98%)
    pallas_call x1, Pallas kernels, per_device(): pl.pallas_call(solve, out_shape=(flat, flat, flat), in_specs=[VMEM] * 6,...  160 us
    pallas_call x1, Pallas kernels, per_device(): pl.pallas_call(arrange, out_shape=(jax.ShapeDtypeStruct((dims, count), F3...  11.1 us
    pallas_call x1, Pallas kernels, per_device(): pl.pallas_call(restore, out_shape=(flat, flat, flat), in_specs=[VMEM] * 5...  10.9 us

profile of v1, /device:TPU:1, one launch (start us, length us, event | category | flops | bytes accessed | tf_op | source)
XLA Modules:
  0.0 184.4 jit_solution(4085790756939280789)
XLA Ops:
  0.6 1.3 copy.13
  1.9 11.1 %shard_map.103 = (f32[16,4096]{1,0:T(8,128)}, f32[16,4096]{1,0:T(8,128)}, f32[16,4096]{1,0:T(8,128)}, s32[32,128]{1,0:T(8,128)}, f32[2,16,256]{2,1,0:T(8,128)}, /*index=5*/f32[16,256]{1,0:T(8,128)}) custom-call(f32[16,4096]{1,0:T(8,128)} %coords.1, f32[16,4096]{1,0:T(8,128)} %resid.1, f32[16,4096]{1,0:T(8,128)} %search.1, s32[32,128]{1,0:T(8,128)} %bitcast.5, ...), custom_call_target="tpu_custom_call" | custom-call | tf_op jit(solution)/shard_map/pallas_call | solution.py:392
  13.0 160.5 %shard_map.104 = (f32[16,4096]{1,0:T(8,128)}, f32[16,4096]{1,0:T(8,128)}, f32[16,4096]{1,0:T(8,128)}) custom-call(f32[16,4096]{1,0:T(8,128)} %get-tuple-element.12.pts, f32[16,4096]{1,0:T(8,128)} %get-tuple-element.13.r_in, f32[16,4096]{1,0:T(8,128)} %get-tuple-element.14.p_in, f32[2,16,256]{2,1,0:T(8,128)} %get-tuple-element.15.skel0, ...), custom_call_target="tpu_custom_call" | custom-call | tf_op jit(solution)/shard_map/pallas_call | solution.py:408
  173.5 10.9 %shard_map.105 = (f32[16,4096]{1,0:T(8,128)}, f32[16,4096]{1,0:T(8,128)}, f32[16,4096]{1,0:T(8,128)}) custom-call(f32[16,4096]{1,0:T(8,128)} %x_in.1, f32[16,4096]{1,0:T(8,128)} %get-tuple-element.17.gain, f32[16,4096]{1,0:T(8,128)} %get-tuple-element.18.resid, f32[16,4096]{1,0:T(8,128)} %get-tuple-element.19.search, s32[32,128]{1,0:T(8,128)} %get-tuple-element.20.inverse), custom_call_target="tpu_custom_call" | custom-call | tf_op jit(solution)/shard_map/pallas_call | solution.py:438

commit v2 on v1

v2 whole, which is shorter than its diff:
```python
import math

import jax
import jax.numpy as jnp
from jax import lax
from jax.experimental import pallas as pl
from jax.experimental.pallas import tpu as pltpu
from jax.sharding import PartitionSpec as P

ITERS = 4
MESH = pl.DeviceIdType.MESH
LANES = 128
LOG2E = math.log2(math.e)
F32 = jnp.float32
BF16 = jnp.bfloat16
VMEM = pl.BlockSpec(memory_space=pltpu.VMEM)

OWN0, OWN1, OWN2, OWN3, UP0, UP1, SIB, COUSIN, UNCLE = range(9)
PER_ROUND = 9


def pick(sources, index_row, first_block, block_count):
    low = index_row & (LANES - 1)
    high = index_row >> 7
    outs = [None] * len(sources)
    for block in range(block_count):
        hit = None
        for n, source in enumerate(sources):
            held = source(first_block + block)
            rows = held.shape[0]
            place = jnp.broadcast_to(low, (rows, LANES))
            got = jnp.take_along_axis(held, place, axis=1, mode="promise_in_bounds")
            if outs[n] is None:
                outs[n] = got
            else:
                hit = jnp.broadcast_to(high, (rows, LANES)) == block
                outs[n] = jnp.where(hit, got, outs[n])
    return outs


def block_of(ref):
    return lambda b: ref[:, b * LANES : (b + 1) * LANES]


def split(value):
    high = value.astype(BF16)
    return high, (value - high.astype(F32)).astype(BF16)


def split3(value):
    high = value.astype(BF16)
    rest = value - high.astype(F32)
    mid = rest.astype(BF16)
    return high, mid, (rest - mid.astype(F32)).astype(BF16)


def mm(a, b):
    return jnp.dot(a, b, preferred_element_type=F32)


def mm_t(a, b):
    return lax.dot_general(a, b, (((1,), (1,)), ((), ())), preferred_element_type=F32)


def stack3(value):
    return jnp.concatenate(split3(value), axis=0)


def fold3(wide):
    rows = wide.shape[0] // 3
    return wide[:rows] + (wide[rows : 2 * rows] + wide[2 * rows :])


def norm_rows(norms, first):
    high, mid, low = (part.astype(F32) for part in split3(norms))
    shape = (16, norms.shape[1])
    row = lax.broadcasted_iota(jnp.int32, shape, 0)
    one = jnp.where((row >= 3 - first) & (row < 6 - first), 1.0, 0.0)
    tile = jnp.where(row == first, high, one)
    tile = jnp.where(row == first + 1, mid, tile)
    return jnp.where(row == first + 2, low, tile)


def left_form(points):
    high, mid, low = (part.astype(F32) for part in split3(points))
    norms = jnp.sum(points * points, axis=0, keepdims=True) * (-LOG2E / 32.0)
    extra = norm_rows(norms, 0)
    full = jnp.concatenate([high, high, mid, mid, high, low, extra, jnp.zeros_like(extra)], axis=0)
    return jnp.transpose(full, (1, 0)).astype(BF16)


def right_form(points):
    high, mid, low = split3(points * (LOG2E / 16.0))
    norms = jnp.sum(points * points, axis=0, keepdims=True) * (-LOG2E / 32.0)
    extra = norm_rows(norms, 3).astype(BF16)
    return jnp.concatenate([high, mid, high, mid, low, high, extra, jnp.zeros_like(extra)], axis=0)


def softmax2(scores, axis):
    weights = jnp.exp2(scores - jnp.max(scores, axis=axis, keepdims=True))
    return weights * (1.0 / jnp.sum(weights, axis=axis, keepdims=True))


def row_dot(a, b):
    return jnp.sum(a * b, axis=1, keepdims=True)


def solve(coords, x_in, r_in, p_in, order, leaf_skel, local_skel, upper, x_out, r_out, p_out,
          near_mat, lefts, rights, ut_hi, ut_lo, t_hi, t_lo, pts, vec, vsplit, image, q_ref, r_ref, p_ref, gain,
          digits, marks, inverse, skel, parent, state, cps,
          points_out, points_in, coef_out, coef_in, line_out, line_in, sum_out, sum_in,
          send_sem, recv_sem, line_send, line_recv):
    me = lax.axis_index("leaf")
    rounds = 4
    line = 16
    leaves, leaf_size = near_mat.shape[0], near_mat.shape[1]
    scale = 1.0 / leaf_size
    rank = parent.shape[1]
    rhs = vec.shape[0]
    local = rounds * PER_ROUND
    blocks = order.shape[0]
    bits = [(me // (1 << u)) % 2 for u in range(2 * rounds)]

    def partner(g, t):
        step = 1 << (2 * g)
        low = (1 - 2 * bits[2 * g]) * step
        high = (1 - 2 * bits[2 * g + 1]) * (2 * step)
        return me + (t % 2) * low + (t // 2) * high

    def on_line(t):
        return me + sum((1 - 2 * bits[u]) * (1 << u) for u in range(4) if t >> u & 1)

    barrier = pltpu.get_barrier_semaphore()
    for t in range(1, line):
        pl.semaphore_signal(barrier, inc=1, device_id=(on_line(t),), device_id_type=MESH)
    for g in range(2, rounds):
        for t in range(1, 4):
            pl.semaphore_signal(barrier, inc=1, device_id=(partner(g, t),), device_id_type=MESH)

    def copies(src, dst, phase, g):
        return [
            pltpu.make_async_remote_copy(
                src_ref=src,
                dst_ref=dst.at[t - 1],
                send_sem=send_sem.at[g, t - 1],
                recv_sem=recv_sem.at[phase, g, t - 1],
                device_id=(partner(g, t),),
                device_id_type=MESH,
            )
            for t in range(1, 4)
        ]

    def line_copies(phase):
        return [
            pltpu.make_async_remote_copy(
                src_ref=line_out,
                dst_ref=line_in.at[phase, t - 1],
                send_sem=line_send.at[t - 1],
                recv_sem=line_recv.at[phase, t - 1],
                device_id=(on_line(t),),
                device_id_type=MESH,
            )
            for t in range(1, line)
        ]

    tile_lane = lax.broadcasted_iota(jnp.int32, (8, LANES), 1)

    def to_tile(column):
        return jnp.where(tile_lane == 0, column[0:8], jnp.where(tile_lane == 1, column[8:16], 0.0))

    def from_tile(tile):
        return jnp.concatenate([tile[:, 0:1], tile[:, 1:2]], axis=0)

    def line_sum(phase):
        parts = [line_out[...]] + [line_in[phase, t] for t in range(line - 1)]
        while len(parts) > 1:
            parts = [a + b for a, b in zip(parts[0::2], parts[1::2])]
        return parts[0]

    def keep(slot, value):
        high, low = split(value)
        t_hi[slot] = high
        t_lo[slot] = low

    def times(stacked, slot):
        return fold3(mm(stacked, t_hi[slot]) + mm(stacked, t_lo[slot]))

    def times_t(stacked, slot):
        return fold3(mm_t(stacked, t_hi[slot]) + mm_t(stacked, t_lo[slot]))

    def choose(first_is_own, index_row, own, other):
        swapped = jnp.where(index_row >= rank, index_row - rank, index_row + rank)
        want = jnp.where(first_is_own, index_row, swapped)
        place = lax.broadcasted_iota(jnp.int32, (rank, rank), 0).astype(F32)
        got = None
        for n, points in enumerate((own, other)):
            hot = jnp.where(place + float(n * rank) == want, 1.0, 0.0).astype(BF16)
            part = fold3(mm(stack3(points), hot))
            got = part if got is None else got + part
        return got

    def place_points(ob, carry):
        row = order[pl.ds(ob, 1), :]
        span = pl.ds(pl.multiple_of(ob * LANES, LANES), LANES)
        pts[:, span] = pick([block_of(coords)], row, 0, blocks)[0]
        place = ob * LANES + lax.broadcasted_iota(jnp.int32, (blocks, LANES), 1)
        hit = lax.broadcasted_iota(jnp.int32, (blocks, LANES), 0) == (row >> 7)
        digits[0:blocks, span] = jnp.where(hit, (place >> 5).astype(F32), 0.0).astype(BF16)
        digits[blocks : 2 * blocks, span] = jnp.where(hit, (place & 31).astype(F32), 0.0).astype(BF16)
        lane_hit = lax.broadcasted_iota(jnp.int32, (LANES, LANES), 0) == (row & (LANES - 1))
        marks[:, span] = jnp.where(lane_hit, 1.0, 0.0).astype(BF16)
        return carry

    lax.fori_loop(0, blocks, place_points, 0)
    leaf_blocks = blocks // leaves
    per = rank // LANES
    for leaf in range(leaves):
        for ob in range(per):
            row = leaf_skel[leaf : leaf + 1, ob * LANES : (ob + 1) * LANES]
            (got,) = pick([block_of(pts)], row, leaf * leaf_blocks, leaf_blocks)
            skel[leaf, :, ob * LANES : (ob + 1) * LANES] = got
    both = lambda b: skel[b // per, :, (b % per) * LANES : (b % per + 1) * LANES]
    for ob in range(per):
        row = local_skel[0:1, ob * LANES : (ob + 1) * LANES]
        (got,) = pick([both], row, 0, 2 * per)
        parent[:, ob * LANES : (ob + 1) * LANES] = got
    pl.semaphore_wait(barrier, line - 1 + 3 * (rounds - 2))

    def place_state():
        sources = [block_of(r_in), block_of(p_in)]

        def body(ob, carry):
            span = pl.ds(pl.multiple_of(ob * LANES, LANES), LANES)
            got = pick(sources, order[pl.ds(ob, 1), :], 0, blocks)
            r_ref[:, span] = got[0]
            vec[:, span] = got[1]
            return carry

        lax.fori_loop(0, blocks, body, 0)
        found = mm_t(digits[...], marks[...])
        inverse[...] = (found[0:blocks] * 32.0 + found[blocks : 2 * blocks]).astype(jnp.int32)

    def make_near():
        for leaf in range(leaves):
            cols = slice(leaf * leaf_size, (leaf + 1) * leaf_size)
            lefts[leaf] = left_form(pts[:, cols])
            rights[:, cols] = right_form(pts[:, cols])

            def body(j, carry, leaf=leaf, cols=cols):
                span = pl.ds(pl.multiple_of(j * rank, rank), rank)
                near_mat[leaf, span, :] = jnp.exp2(mm(lefts[leaf, span, :], rights[:, cols])).astype(BF16)
                return carry

            lax.fori_loop(0, leaf_size // rank, body, 0)

    def make_basis(leaf):
        left = left_form(skel[leaf])

        def body(j, carry):
            inner = pl.ds(pl.multiple_of(j * rank, rank), rank)
            span = pl.ds(pl.multiple_of(leaf * leaf_size + j * rank, rank), rank)
            high, low = split(softmax2(mm(left, rights[:, span]), 0))
            ut_hi[leaf, :, inner] = high
            ut_lo[leaf, :, inner] = low
            return carry

        lax.fori_loop(0, leaf_size // rank, body, 0)

    def make_local():
        skel_left = [left_form(skel[leaf]) for leaf in range(leaves)]
        parent_right = right_form(parent[...])
        for leaf in range(leaves):
            keep(local + leaf, softmax2(mm(skel_left[leaf], parent_right), 1))
        keep(local + 2, jnp.exp2(mm(skel_left[0], right_form(skel[1]))) * scale)

    beside = [place_state, make_near, lambda: make_basis(0), lambda: make_basis(1)]
    later = make_local
    own = parent[...]
    for g in range(rounds):
        u = 2 * g
        points_out[g, 0:16, :] = own
        points_out[g, 16:24, :] = jnp.broadcast_to(upper[u : u + 1, :].astype(F32), (8, rank))
        sends = copies(points_out.at[g], points_in.at[g], 0, g)
        for c in sends:
            c.start()
        later()
        beside[g]()
        for c in sends:
            c.wait()
        low = [own] + [points_in[g, t, 0:16, :] for t in range(3)]
        lists = [points_out[g, 16:17, :], points_in[g, 1, 16:17, :]]
        mids = [choose(bits[u] == 0, lists[n], low[2 * n], low[2 * n + 1]) for n in range(2)]
        top = None
        if g + 1 < rounds:
            top = choose(bits[u + 1] == 0, upper[u + 1 : u + 2, :].astype(F32), mids[0], mids[1])

        def later(base=g * PER_ROUND, low=low, mids=mids, top=top):
            low_left = [left_form(x) for x in low]
            mid_left = [left_form(x) for x in mids]
            mid_right = [right_form(x) for x in mids]
            for t in range(4):
                keep(base + OWN0 + t, softmax2(mm(low_left[t], mid_right[t // 2]), 1))
            keep(base + SIB, jnp.exp2(mm(low_left[1], right_form(low[0]))) * scale)
            keep(base + COUSIN, jnp.exp2(mm(low_left[3], right_form(low[2]))) * scale)
            keep(base + UNCLE, jnp.exp2(mm(mid_left[1], mid_right[0])) * scale)
            if top is not None:
                top_right = right_form(top)
                for n in range(2):
                    keep(base + UP0 + n, softmax2(mm(mid_left[n], top_right), 1))

        own = top
    later()

    p_ref[...] = jnp.zeros_like(p_ref)
    q_ref[...] = jnp.zeros_like(q_ref)
    gain[...] = jnp.zeros_like(gain)
    state[0] = jnp.ones(state.shape[1:], F32)
    state[1] = jnp.zeros(state.shape[1:], F32)
    lane = lax.broadcasted_iota(jnp.int32, (rhs, LANES), 1)

    def near_product(leaf):
        def body(j, carry):
            inner = pl.ds(pl.multiple_of(j * rank, rank), rank)
            span = pl.ds(pl.multiple_of(leaf * leaf_size + j * rank, rank), rank)
            wide = fold3(mm(vsplit[:, leaf * leaf_size : (leaf + 1) * leaf_size], near_mat[leaf, :, inner]))
            image[:, span] = 0.5 * vec[:, span] + wide * scale
            return carry

        lax.fori_loop(0, leaf_size // rank, body, 0)

    def iteration(k, carry):
        vsplit[...] = stack3(vec[...])
        leaf_coef = []
        for leaf in range(leaves):
            part = vsplit[:, leaf * leaf_size : (leaf + 1) * leaf_size]
            leaf_coef.append(fold3(mm_t(part, ut_hi[leaf]) + mm_t(part, ut_lo[leaf])))
        wide = [stack3(x) for x in leaf_coef]
        coef = times(wide[0], local) + times(wide[1], local + 1)
        leaf_cp = [times_t(wide[1], local + 2), times(wide[0], local + 2)]
        sums = jnp.where(lane == 0, row_dot(r_ref[...], r_ref[...]), 0.0)
        sums = jnp.where(lane == 1, row_dot(r_ref[...], q_ref[...]), sums)
        sums = jnp.where(lane == 2, 2.0 * row_dot(leaf_coef[0], leaf_cp[0]), sums)
        for g in range(rounds):
            base = g * PER_ROUND
            if g == 2:
                sums = jnp.where(lane == 3, row_dot(vec[...], image[...]), sums)
            coef_out[g, :, 0:rank] = coef
            coef_out[g, :, rank : rank + LANES] = sums
            sends = copies(coef_out.at[g], coef_in.at[k, g], 1 + k, g)
            for c in sends:
                c.start()
            if g < leaves:
                near_product(g)
            for c in sends:
                c.wait()
            got = [coef] + [coef_in[k, g, t, :, 0:rank] for t in range(3)]
            far = [coef_in[k, g, t, :, rank : rank + LANES] for t in range(3)]
            wide = [stack3(x) for x in got]
            mid0 = times(wide[0], base + OWN0) + times(wide[1], base + OWN1)
            mid1 = times(wide[2], base + OWN2) + times(wide[3], base + OWN3)
            mid1_wide = stack3(mid1)
            if g + 1 < rounds:
                coef = times(stack3(mid0), base + UP0) + times(mid1_wide, base + UP1)
            low_cp = times(wide[1], base + SIB)
            mid_cp = times(mid1_wide, base + UNCLE)
            cps[2 * g] = low_cp
            cps[2 * g + 1] = mid_cp
            quad = row_dot(got[0], low_cp) + row_dot(got[2], times(wide[3], base + COUSIN)) + row_dot(mid0, mid_cp)
            sums = (sums + far[0]) + (far[1] + far[2]) + jnp.where(lane == 2, 2.0 * quad, 0.0)
        line_out[...] = to_tile(sums[:, 3:4])
        sends = line_copies(k)
        for c in sends:
            c.start()
        down = cps[2 * rounds - 1]
        for u in range(2 * rounds - 2, -1, -1):
            down = cps[u] + times_t(stack3(down), (u // 2) * PER_ROUND + (UP0 if u % 2 else OWN0))
        down_wide = stack3(down)
        for leaf in range(leaves):
            cols = slice(leaf * leaf_size, (leaf + 1) * leaf_size)
            part = stack3(leaf_cp[leaf] + times_t(down_wide, local + leaf))
            image[:, cols] += fold3(mm(part, ut_hi[leaf]) + mm(part, ut_lo[leaf]))
        for c in sends:
            c.wait()
        near = from_tile(line_sum(k))
        fresh = sums[:, 0:1]
        cross = sums[:, 1:2]
        beta = fresh / state[0, :, 0:1]
        curve = (sums[:, 2:3] + near) + 2.0 * beta * cross + beta * beta * state[1, :, 0:1]
        alpha = fresh / curve
        state[0] = jnp.broadcast_to(fresh, (rhs, LANES))
        state[1] = jnp.broadcast_to(curve, (rhs, LANES))
        p_new = vec[...] + beta * p_ref[...]
        q_new = image[...] + beta * q_ref[...]
        p_ref[...] = p_new
        q_ref[...] = q_new
        gain[...] += alpha * p_new
        r_new = r_ref[...] - alpha * q_new
        r_ref[...] = r_new
        vec[...] = r_new
        return carry

    lax.fori_loop(0, ITERS, iteration, 0)

    sources = [block_of(gain), block_of(r_ref), block_of(p_ref)]

    def restore(ob, carry):
        span = pl.ds(pl.multiple_of(ob * LANES, LANES), LANES)
        got = pick(sources, inverse[pl.ds(ob, 1), :], 0, blocks)
        x_out[:, span] = x_in[:, span] + got[0]
        r_out[:, span] = got[1]
        p_out[:, span] = got[2]
        return carry

    line_out[...] = to_tile(row_dot(r_ref[...], r_ref[...]))
    sends = line_copies(ITERS)
    for c in sends:
        c.start()
    cut = [0, blocks * 7 // 16, blocks * 23 // 32, blocks]
    lax.fori_loop(cut[0], cut[1], restore, 0)
    for c in sends:
        c.wait()
    tile = line_sum(ITERS)
    for g in range(2, rounds):
        sum_out[g - 2] = tile
        sends = copies(sum_out.at[g - 2], sum_in.at[g - 2], 1 + ITERS, g)
        for c in sends:
            c.start()
        lax.fori_loop(cut[g - 1], cut[g], restore, 0)
        for c in sends:
            c.wait()
        tile = (tile + sum_in[g - 2, 0]) + (sum_in[g - 2, 1] + sum_in[g - 2, 2])
    p_out[...] = r_out[...] + from_tile(tile) / state[0, :, 0:1] * p_out[...]


def per_device(coords, solution, residual, direction, order, leaf_skel, local_skel, upper_skel):
    dims, count = coords.shape
    rhs = solution.shape[0]
    leaves, rank = leaf_skel.shape
    leaf_size = count // leaves
    blocks = count // LANES
    flat = jax.ShapeDtypeStruct((rhs, count), F32)
    slots = 4 * PER_ROUND + 3
    return pl.pallas_call(
        solve,
        out_shape=(flat, flat, flat),
        in_specs=[VMEM] * 8,
        out_specs=(VMEM,) * 3,
        scratch_shapes=[
            pltpu.VMEM((leaves, leaf_size, leaf_size), BF16),
            pltpu.VMEM((leaves, leaf_size, LANES), BF16),
            pltpu.VMEM((LANES, count), BF16),
            pltpu.VMEM((leaves, rank, leaf_size), BF16),
            pltpu.VMEM((leaves, rank, leaf_size), BF16),
            pltpu.VMEM((slots, rank, rank), BF16),
            pltpu.VMEM((slots, rank, rank), BF16),
            pltpu.VMEM((dims, count), F32),
            pltpu.VMEM((rhs, count), F32),
            pltpu.VMEM((3 * rhs, count), BF16),
            pltpu.VMEM((rhs, count), F32),
            pltpu.VMEM((rhs, count), F32),
            pltpu.VMEM((rhs, count), F32),
            pltpu.VMEM((rhs, count), F32),
            pltpu.VMEM((rhs, count), F32),
            pltpu.VMEM((2 * blocks, count), BF16),
            pltpu.VMEM((LANES, count), BF16),
            pltpu.VMEM((blocks, LANES), jnp.int32),
            pltpu.VMEM((leaves, dims, rank), F32),
            pltpu.VMEM((dims, rank), F32),
            pltpu.VMEM((2, rhs, LANES), F32),
            pltpu.VMEM((8, rhs, rank), F32),
            pltpu.VMEM((4, dims + 8, rank), F32),
            pltpu.VMEM((4, 3, dims + 8, rank), F32),
            pltpu.VMEM((4, rhs, rank + LANES), F32),
            pltpu.VMEM((ITERS, 4, 3, rhs, rank + LANES), F32),
            pltpu.VMEM((8, LANES), F32),
            pltpu.VMEM((ITERS + 1, 15, 8, LANES), F32),
            pltpu.VMEM((2, 8, LANES), F32),
            pltpu.VMEM((2, 3, 8, LANES), F32),
            pltpu.SemaphoreType.DMA((4, 3)),
            pltpu.SemaphoreType.DMA((ITERS + 2, 4, 3)),
            pltpu.SemaphoreType.DMA((15,)),
            pltpu.SemaphoreType.DMA((ITERS + 1, 15)),
        ],
        compiler_params=pltpu.CompilerParams(
            vmem_limit_bytes=56 * 1024 * 1024, collective_id=0, has_side_effects=True
        ),
    )(
        coords,
        solution,
        residual,
        direction,
        order.reshape(blocks, LANES),
        leaf_skel,
        local_skel,
        jnp.swapaxes(upper_skel, 0, 1).reshape(-1, rank),
    )


def solution(mesh):
    in_specs = (
        P(None, "leaf"),
        P(None, "leaf"),
        P(None, "leaf"),
        P(None, "leaf"),
        P("leaf"),
        P("leaf", None),
        P("leaf", None),
        P(None, "leaf", None),
    )
    out_specs = (P(None, "leaf"), P(None, "leaf"), P(None, "leaf"))
    return jax.shard_map(
        per_device, mesh=mesh, in_specs=in_specs, out_specs=out_specs, check_vma=False
    )
```

time: 185 us -> 161 us (0.87)
  Pallas kernels: 182 us -> 156 us
  local copies, waits for them, and re-layouts: 1.29 us -> 4.76 us
    pallas_call x3 -> x1, Pallas kernels: 182 us -> 156 us  [per_device(): pl.pallas_call(solve, out_shape=(flat, flat, flat), in_specs=[VMEM] * 8,...]
    unnamed x1 -> x8, local copies, waits for them, and re-layouts: 1.29 us -> 4.76 us
where the time goes in v2:
time: 161 us
  Pallas kernels  156 us (97%)
  local copies, waits for them, and re-layouts  4.76 us (3%)
    pallas_call x1, Pallas kernels, per_device(): pl.pallas_call(solve, out_shape=(flat, flat, flat), in_specs=[VMEM] * 8,...  156 us
    unnamed x8, local copies, waits for them, and re-layouts  4.76 us

profile of v2, /device:TPU:1, one launch (start us, length us, event | category | flops | bytes accessed | tf_op | source)
XLA Modules:
  0.0 161.0 jit_solution(2569765023635300046)
XLA Ops:
  0.6 1.3 copy.13
  1.9 155.6 %shard_map.103 = (f32[16,4096]{1,0:T(8,128)}, f32[16,4096]{1,0:T(8,128)}, f32[16,4096]{1,0:T(8,128)}) custom-call(f32[16,4096]{1,0:T(8,128)} %coords.1, f32[16,4096]{1,0:T(8,128)} %x_in.1, f32[16,4096]{1,0:T(8,128)} %r_in.1, f32[16,4096]{1,0:T(8,128)} %p_in.1, s32[32,128]{1,0:T(8,128)} %bitcast.5, s32[2,256]{1,0:T(2,128)} %leaf_skel.1, s32[1,256]{1,0:T(1,128)} %local_skel.1, ...), custom_call_target="tpu_custom_call" | custom-call | tf_op jit(solution)/shard_map/pallas_call | solution.py:443
  157.6 0.0 copy-start.1
  157.6 1.7 %copy.17 = f32[16,4096]{1,0:T(8,128)} copy(f32[16,4096]{1,0:T(8,128)} %get-tuple-element.6) | data formatting | bytes 524288
  159.3 0.0 copy-done.1
  159.3 0.0 copy-start
  159.3 0.7 copy.18
  160.0 0.3 copy-done
  160.3 0.7 copy.19
Async XLA Ops:
  157.6 1.7 %copy-start.1 = (f32[16,4096]{1,0:T(8,128)S(1)}, f32[16,4096]{1,0:T(8,128)}, u32[]{:S(2)}) copy-start(f32[16,4096]{1,0:T(8,128)} %get-tuple-element.7) | copy-start | bytes 786436
  159.3 1.0 copy-start

commit v3 on v2

--- a/solution.py
+++ b/solution.py
@@ -108,8 +108,8 @@
 def solve(coords, x_in, r_in, p_in, order, leaf_skel, local_skel, upper, x_out, r_out, p_out,
           near_mat, lefts, rights, ut_hi, ut_lo, t_hi, t_lo, pts, vec, vsplit, image, q_ref, r_ref, p_ref, gain,
           digits, marks, inverse, skel, parent, state, cps,
-          points_out, points_in, coef_out, coef_in, line_out, line_in, sum_out, sum_in,
-          send_sem, recv_sem, line_send, line_recv):
+          points_out, points_in, coef_out, coef_in, sums_out, sums_in, middles, line_out, line_in, plane_in, tile_out, tile_in,
+          send_sem, recv_sem, sums_send, sums_recv, line_send, line_recv, plane_recv, tile_send, tile_recv):
     me = lax.axis_index("leaf")
     rounds = 4
     line = 16
@@ -130,20 +130,21 @@
     def on_line(t):
         return me + sum((1 - 2 * bits[u]) * (1 << u) for u in range(4) if t >> u & 1)
 
+    def on_plane(t):
+        return me + sum((1 - 2 * bits[u + 4]) * (1 << (u + 4)) for u in range(4) if t >> u & 1)
+
     barrier = pltpu.get_barrier_semaphore()
     for t in range(1, line):
         pl.semaphore_signal(barrier, inc=1, device_id=(on_line(t),), device_id_type=MESH)
-    for g in range(2, rounds):
-        for t in range(1, 4):
-            pl.semaphore_signal(barrier, inc=1, device_id=(partner(g, t),), device_id_type=MESH)
-
-    def copies(src, dst, phase, g):
+        pl.semaphore_signal(barrier, inc=1, device_id=(on_plane(t),), device_id_type=MESH)
+
+    def copies(src, dst, sent, received, g):
         return [
             pltpu.make_async_remote_copy(
                 src_ref=src,
                 dst_ref=dst.at[t - 1],
-                send_sem=send_sem.at[g, t - 1],
-                recv_sem=recv_sem.at[phase, g, t - 1],
+                send_sem=sent.at[t - 1],
+                recv_sem=received.at[t - 1],
                 device_id=(partner(g, t),),
                 device_id_type=MESH,
             )
@@ -163,6 +164,19 @@
             for t in range(1, line)
         ]
 
+    def plane_copies():
+        return [
+            pltpu.make_async_remote_copy(
+                src_ref=line_out,
+                dst_ref=plane_in.at[t - 1],
+                send_sem=line_send.at[t - 1],
+                recv_sem=plane_recv.at[t - 1],
+                device_id=(on_plane(t),),
+                device_id_type=MESH,
+            )
+            for t in range(1, line)
+        ]
+
     tile_lane = lax.broadcasted_iota(jnp.int32, (8, LANES), 1)
 
     def to_tile(column):
@@ -171,8 +185,14 @@
     def from_tile(tile):
         return jnp.concatenate([tile[:, 0:1], tile[:, 1:2]], axis=0)
 
-    def line_sum(phase):
-        parts = [line_out[...]] + [line_in[phase, t] for t in range(line - 1)]
+    def tile_copies(phase, n):
+        return copies(tile_out.at[n], tile_in.at[phase, n], tile_send.at[n], tile_recv.at[phase, n], n + 2)
+
+    def tile_sum(phase, n):
+        return (tile_out[n] + tile_in[phase, n, 0]) + (tile_in[phase, n, 1] + tile_in[phase, n, 2])
+
+    def line_sum(got):
+        parts = [line_out[...]] + [got[t] for t in range(line - 1)]
         while len(parts) > 1:
             parts = [a + b for a, b in zip(parts[0::2], parts[1::2])]
         return parts[0]
@@ -211,7 +231,7 @@
         marks[:, span] = jnp.where(lane_hit, 1.0, 0.0).astype(BF16)
         return carry
 
-    lax.fori_loop(0, blocks, place_points, 0)
+    lax.fori_loop(0, blocks // 4, lambda group, carry: [place_points(group * 4 + n, carry) for n in range(4)][-1], 0)
     leaf_blocks = blocks // leaves
     per = rank // LANES
     for leaf in range(leaves):
@@ -224,19 +244,21 @@
         row = local_skel[0:1, ob * LANES : (ob + 1) * LANES]
         (got,) = pick([both], row, 0, 2 * per)
         parent[:, ob * LANES : (ob + 1) * LANES] = got
-    pl.semaphore_wait(barrier, line - 1 + 3 * (rounds - 2))
+    pl.semaphore_wait(barrier, 2 * (line - 1))
 
     def place_state():
         sources = [block_of(r_in), block_of(p_in)]
 
-        def body(ob, carry):
-            span = pl.ds(pl.multiple_of(ob * LANES, LANES), LANES)
-            got = pick(sources, order[pl.ds(ob, 1), :], 0, blocks)
-            r_ref[:, span] = got[0]
-            vec[:, span] = got[1]
+        def body(group, carry):
+            for n in range(4):
+                ob = group * 4 + n
+                span = pl.ds(pl.multiple_of(ob * LANES, LANES), LANES)
+                got = pick(sources, order[pl.ds(ob, 1), :], 0, blocks)
+                r_ref[:, span] = got[0]
+                vec[:, span] = got[1]
             return carry
 
-        lax.fori_loop(0, blocks, body, 0)
+        lax.fori_loop(0, blocks // 4, body, 0)
         found = mm_t(digits[...], marks[...])
         inverse[...] = (found[0:blocks] * 32.0 + found[blocks : 2 * blocks]).astype(jnp.int32)
 
@@ -256,15 +278,17 @@
     def make_basis(leaf):
         left = left_form(skel[leaf])
 
-        def body(j, carry):
-            inner = pl.ds(pl.multiple_of(j * rank, rank), rank)
-            span = pl.ds(pl.multiple_of(leaf * leaf_size + j * rank, rank), rank)
-            high, low = split(softmax2(mm(left, rights[:, span]), 0))
-            ut_hi[leaf, :, inner] = high
-            ut_lo[leaf, :, inner] = low
+        def body(group, carry):
+            for n in range(4):
+                j = group * 4 + n
+                inner = pl.ds(pl.multiple_of(j * rank, rank), rank)
+                span = pl.ds(pl.multiple_of(leaf * leaf_size + j * rank, rank), rank)
+                high, low = split(softmax2(mm(left, rights[:, span]), 0))
+                ut_hi[leaf, :, inner] = high
+                ut_lo[leaf, :, inner] = low
             return carry
 
-        lax.fori_loop(0, leaf_size // rank, body, 0)
+        lax.fori_loop(0, leaf_size // rank // 4, body, 0)
 
     def make_local():
         skel_left = [left_form(skel[leaf]) for leaf in range(leaves)]
@@ -273,49 +297,55 @@
             keep(local + leaf, softmax2(mm(skel_left[leaf], parent_right), 1))
         keep(local + 2, jnp.exp2(mm(skel_left[0], right_form(skel[1]))) * scale)
 
-    beside = [place_state, make_near, lambda: make_basis(0), lambda: make_basis(1)]
-    later = make_local
+    def make_round(g):
+        base = g * PER_ROUND
+        low = [points_out[g, 0:16, :]] + [points_in[g, t, 0:16, :] for t in range(3)]
+        mids = [middles[g, n] for n in range(2)]
+        low_left = [left_form(x) for x in low]
+        mid_left = [left_form(x) for x in mids]
+        mid_right = [right_form(x) for x in mids]
+        for t in range(4):
+            keep(base + OWN0 + t, softmax2(mm(low_left[t], mid_right[t // 2]), 1))
+        keep(base + SIB, jnp.exp2(mm(low_left[1], right_form(low[0]))) * scale)
+        keep(base + COUSIN, jnp.exp2(mm(low_left[3], right_form(low[2]))) * scale)
+        keep(base + UNCLE, jnp.exp2(mm(mid_left[1], mid_right[0])) * scale)
+        if g + 1 < rounds:
+            top_right = right_form(points_out[g + 1, 0:16, :])
+            for n in range(2):
+                keep(base + UP0 + n, softmax2(mm(mid_left[n], top_right), 1))
+
+    beside = [
+        (place_state,),
+        (make_near,),
+        (lambda: make_basis(0), lambda: make_round(0)),
+        (lambda: make_basis(1), lambda: make_round(1), make_local),
+    ]
     own = parent[...]
     for g in range(rounds):
         u = 2 * g
         points_out[g, 0:16, :] = own
-        points_out[g, 16:24, :] = jnp.broadcast_to(upper[u : u + 1, :].astype(F32), (8, rank))
-        sends = copies(points_out.at[g], points_in.at[g], 0, g)
+        points_out[g, 16:24, :] = jnp.broadcast_to(upper[u].astype(F32), (8, rank))
+        sends = copies(points_out.at[g], points_in.at[g], send_sem.at[g], recv_sem.at[0, g], g)
         for c in sends:
             c.start()
-        later()
-        beside[g]()
+        for work in beside[g]:
+            work()
         for c in sends:
             c.wait()
         low = [own] + [points_in[g, t, 0:16, :] for t in range(3)]
         lists = [points_out[g, 16:17, :], points_in[g, 1, 16:17, :]]
         mids = [choose(bits[u] == 0, lists[n], low[2 * n], low[2 * n + 1]) for n in range(2)]
-        top = None
+        for n in range(2):
+            middles[g, n] = mids[n]
         if g + 1 < rounds:
-            top = choose(bits[u + 1] == 0, upper[u + 1 : u + 2, :].astype(F32), mids[0], mids[1])
-
-        def later(base=g * PER_ROUND, low=low, mids=mids, top=top):
-            low_left = [left_form(x) for x in low]
-            mid_left = [left_form(x) for x in mids]
-            mid_right = [right_form(x) for x in mids]
-            for t in range(4):
-                keep(base + OWN0 + t, softmax2(mm(low_left[t], mid_right[t // 2]), 1))
-            keep(base + SIB, jnp.exp2(mm(low_left[1], right_form(low[0]))) * scale)
-            keep(base + COUSIN, jnp.exp2(mm(low_left[3], right_form(low[2]))) * scale)
-            keep(base + UNCLE, jnp.exp2(mm(mid_left[1], mid_right[0])) * scale)
-            if top is not None:
-                top_right = right_form(top)
-                for n in range(2):
-                    keep(base + UP0 + n, softmax2(mm(mid_left[n], top_right), 1))
-
-        own = top
-    later()
+            own = choose(bits[u + 1] == 0, upper[u + 1].astype(F32), mids[0], mids[1])
 
     p_ref[...] = jnp.zeros_like(p_ref)
     q_ref[...] = jnp.zeros_like(q_ref)
     gain[...] = jnp.zeros_like(gain)
     state[0] = jnp.ones(state.shape[1:], F32)
     state[1] = jnp.zeros(state.shape[1:], F32)
+    state[2] = jnp.zeros(state.shape[1:], F32)
     lane = lax.broadcasted_iota(jnp.int32, (rhs, LANES), 1)
 
     def near_product(leaf):
@@ -336,41 +366,64 @@
             leaf_coef.append(fold3(mm_t(part, ut_hi[leaf]) + mm_t(part, ut_lo[leaf])))
         wide = [stack3(x) for x in leaf_coef]
         coef = times(wide[0], local) + times(wide[1], local + 1)
-        leaf_cp = [times_t(wide[1], local + 2), times(wide[0], local + 2)]
-        sums = jnp.where(lane == 0, row_dot(r_ref[...], r_ref[...]), 0.0)
-        sums = jnp.where(lane == 1, row_dot(r_ref[...], q_ref[...]), sums)
-        sums = jnp.where(lane == 2, 2.0 * row_dot(leaf_coef[0], leaf_cp[0]), sums)
+        last = None
         for g in range(rounds):
             base = g * PER_ROUND
-            if g == 2:
-                sums = jnp.where(lane == 3, row_dot(vec[...], image[...]), sums)
-            coef_out[g, :, 0:rank] = coef
-            coef_out[g, :, rank : rank + LANES] = sums
-            sends = copies(coef_out.at[g], coef_in.at[k, g], 1 + k, g)
+            coef_out[g] = coef
+            sends = copies(coef_out.at[g], coef_in.at[k, g], send_sem.at[g], recv_sem.at[1 + k, g], g)
             for c in sends:
+                c.start()
+            if g == 0:
+                leaf_cp = [times_t(wide[1], local + 2), times(wide[0], local + 2)]
+                sums = jnp.where(lane == 0, row_dot(r_ref[...], r_ref[...]), 0.0)
+                sums = jnp.where(lane == 1, row_dot(vec[...], q_ref[...]), sums)
+                sums = jnp.where(lane == 3, row_dot(r_ref[...], vec[...]), sums)
+                sums = jnp.where(lane == 4, row_dot(vec[...], vec[...]), sums)
+                sums = jnp.where(lane == 2, 2.0 * row_dot(leaf_coef[0], leaf_cp[0]), sums)
+            else:
+                sums = last()
+            sums_out[g] = sums
+            sum_sends = copies(sums_out.at[g], sums_in.at[k, g], sums_send.at[g], sums_recv.at[k, g], g)
+            for c in sum_sends:
                 c.start()
             if g < leaves:
                 near_product(g)
+            if g == 1:
+                line_out[...] = to_tile(row_dot(vec[...], image[...]))
+                side = line_copies(k)
+            else:
+                if g > 1:
+                    for c in side:
+                        c.wait()
+                    tile_out[g - 2] = line_sum(line_in.at[k]) if g == 2 else tile_sum(k, 0)
+                    side = tile_copies(k, g - 2)
+            if g > 0:
+                for c in side:
+                    c.start()
+            if g in (1, 2):
+                pl.when(k == 0)(lambda g=g: make_round(g + 1))
             for c in sends:
                 c.wait()
-            got = [coef] + [coef_in[k, g, t, :, 0:rank] for t in range(3)]
-            far = [coef_in[k, g, t, :, rank : rank + LANES] for t in range(3)]
+            got = [coef] + [coef_in[k, g, t] for t in range(3)]
             wide = [stack3(x) for x in got]
             mid0 = times(wide[0], base + OWN0) + times(wide[1], base + OWN1)
             mid1 = times(wide[2], base + OWN2) + times(wide[3], base + OWN3)
             mid1_wide = stack3(mid1)
             if g + 1 < rounds:
                 coef = times(stack3(mid0), base + UP0) + times(mid1_wide, base + UP1)
-            low_cp = times(wide[1], base + SIB)
-            mid_cp = times(mid1_wide, base + UNCLE)
-            cps[2 * g] = low_cp
-            cps[2 * g + 1] = mid_cp
-            quad = row_dot(got[0], low_cp) + row_dot(got[2], times(wide[3], base + COUSIN)) + row_dot(mid0, mid_cp)
-            sums = (sums + far[0]) + (far[1] + far[2]) + jnp.where(lane == 2, 2.0 * quad, 0.0)
-        line_out[...] = to_tile(sums[:, 3:4])
-        sends = line_copies(k)
-        for c in sends:
-            c.start()
+
+            def last(g=g, base=base, got=got, wide=wide, mid0=mid0, mid1_wide=mid1_wide, sums=sums, sent=sum_sends):
+                low_cp = times(wide[1], base + SIB)
+                mid_cp = times(mid1_wide, base + UNCLE)
+                cps[2 * g] = low_cp
+                cps[2 * g + 1] = mid_cp
+                quad = row_dot(got[0], low_cp) + row_dot(got[2], times(wide[3], base + COUSIN)) + row_dot(mid0, mid_cp)
+                for c in sent:
+                    c.wait()
+                far = [sums_in[k, g, t] for t in range(3)]
+                return (sums + far[0]) + (far[1] + far[2]) + jnp.where(lane == 2, 2.0 * quad, 0.0)
+
+        sums = last()
         down = cps[2 * rounds - 1]
         for u in range(2 * rounds - 2, -1, -1):
             down = cps[u] + times_t(stack3(down), (u // 2) * PER_ROUND + (UP0 if u % 2 else OWN0))
@@ -379,12 +432,14 @@
             cols = slice(leaf * leaf_size, (leaf + 1) * leaf_size)
             part = stack3(leaf_cp[leaf] + times_t(down_wide, local + leaf))
             image[:, cols] += fold3(mm(part, ut_hi[leaf]) + mm(part, ut_lo[leaf]))
-        for c in sends:
+        for c in side:
             c.wait()
-        near = from_tile(line_sum(k))
+        near = from_tile(tile_sum(k, 1))
         fresh = sums[:, 0:1]
         cross = sums[:, 1:2]
-        beta = fresh / state[0, :, 0:1]
+        beta = fresh / state[0, :, 0:1] - state[2, :, 0:1]
+        guess = jnp.where(k == 0, 1.0 + (fresh - 2.0 * sums[:, 3:4]) / sums[:, 4:5], 0.0)
+        state[2] = jnp.broadcast_to(guess, (rhs, LANES))
         curve = (sums[:, 2:3] + near) + 2.0 * beta * cross + beta * beta * state[1, :, 0:1]
         alpha = fresh / curve
         state[0] = jnp.broadcast_to(fresh, (rhs, LANES))
@@ -396,39 +451,38 @@
         gain[...] += alpha * p_new
         r_new = r_ref[...] - alpha * q_new
         r_ref[...] = r_new
-        vec[...] = r_new
+        vec[...] = r_new + guess * p_new
         return carry
 
     lax.fori_loop(0, ITERS, iteration, 0)
 
     sources = [block_of(gain), block_of(r_ref), block_of(p_ref)]
 
-    def restore(ob, carry):
-        span = pl.ds(pl.multiple_of(ob * LANES, LANES), LANES)
-        got = pick(sources, inverse[pl.ds(ob, 1), :], 0, blocks)
-        x_out[:, span] = x_in[:, span] + got[0]
-        r_out[:, span] = got[1]
-        p_out[:, span] = got[2]
+    def restore(group, carry):
+        for n in range(4):
+            ob = group * 4 + n
+            span = pl.ds(pl.multiple_of(ob * LANES, LANES), LANES)
+            got = pick(sources, inverse[pl.ds(ob, 1), :], 0, blocks)
+            x_out[:, span] = x_in[:, span] + got[0]
+            r_out[:, span] = got[1]
+            p_out[:, span] = got[2]
         return carry
 
     line_out[...] = to_tile(row_dot(r_ref[...], r_ref[...]))
     sends = line_copies(ITERS)
     for c in sends:
         c.start()
-    cut = [0, blocks * 7 // 16, blocks * 23 // 32, blocks]
-    lax.fori_loop(cut[0], cut[1], restore, 0)
+    lax.fori_loop(0, blocks // 8, restore, 0)
     for c in sends:
         c.wait()
-    tile = line_sum(ITERS)
-    for g in range(2, rounds):
-        sum_out[g - 2] = tile
-        sends = copies(sum_out.at[g - 2], sum_in.at[g - 2], 1 + ITERS, g)
-        for c in sends:
-            c.start()
-        lax.fori_loop(cut[g - 1], cut[g], restore, 0)
-        for c in sends:
-            c.wait()
-        tile = (tile + sum_in[g - 2, 0]) + (sum_in[g - 2, 1] + sum_in[g - 2, 2])
+    line_out[...] = line_sum(line_in.at[ITERS])
+    sends = plane_copies()
+    for c in sends:
+        c.start()
+    lax.fori_loop(blocks // 8, blocks // 4, restore, 0)
+    for c in sends:
+        c.wait()
+    tile = line_sum(plane_in)
     p_out[...] = r_out[...] + from_tile(tile) / state[0, :, 0:1] * p_out[...]
 
 
@@ -466,20 +520,29 @@
             pltpu.VMEM((blocks, LANES), jnp.int32),
             pltpu.VMEM((leaves, dims, rank), F32),
             pltpu.VMEM((dims, rank), F32),
-            pltpu.VMEM((2, rhs, LANES), F32),
+            pltpu.VMEM((3, rhs, LANES), F32),
             pltpu.VMEM((8, rhs, rank), F32),
             pltpu.VMEM((4, dims + 8, rank), F32),
             pltpu.VMEM((4, 3, dims + 8, rank), F32),
-            pltpu.VMEM((4, rhs, rank + LANES), F32),
-            pltpu.VMEM((ITERS, 4, 3, rhs, rank + LANES), F32),
+            pltpu.VMEM((4, rhs, rank), F32),
+            pltpu.VMEM((ITERS, 4, 3, rhs, rank), F32),
+            pltpu.VMEM((4, rhs, LANES), F32),
+            pltpu.VMEM((ITERS, 4, 3, rhs, LANES), F32),
+            pltpu.VMEM((4, 2, dims, rank), F32),
             pltpu.VMEM((8, LANES), F32),
             pltpu.VMEM((ITERS + 1, 15, 8, LANES), F32),
+            pltpu.VMEM((15, 8, LANES), F32),
             pltpu.VMEM((2, 8, LANES), F32),
-            pltpu.VMEM((2, 3, 8, LANES), F32),
+            pltpu.VMEM((ITERS, 2, 3, 8, LANES), F32),
             pltpu.SemaphoreType.DMA((4, 3)),
-            pltpu.SemaphoreType.DMA((ITERS + 2, 4, 3)),
+            pltpu.SemaphoreType.DMA((ITERS + 1, 4, 3)),
+            pltpu.SemaphoreType.DMA((4, 3)),
+            pltpu.SemaphoreType.DMA((ITERS, 4, 3)),
             pltpu.SemaphoreType.DMA((15,)),
             pltpu.SemaphoreType.DMA((ITERS + 1, 15)),
+            pltpu.SemaphoreType.DMA((15,)),
+            pltpu.SemaphoreType.DMA((2, 3)),
+            pltpu.SemaphoreType.DMA((ITERS, 2, 3)),
         ],
         compiler_params=pltpu.CompilerParams(
             vmem_limit_bytes=56 * 1024 * 1024, collective_id=0, has_side_effects=True
@@ -492,7 +555,7 @@
         order.reshape(blocks, LANES),
         leaf_skel,
         local_skel,
-        jnp.swapaxes(upper_skel, 0, 1).reshape(-1, rank),
+        upper_skel,
     )
 
 

time: 161 us -> 140 us (0.87)
  Pallas kernels: 156 us -> 136 us
    pallas_call x1, Pallas kernels: 156 us -> 136 us  [per_device(): pl.pallas_call(solve, out_shape=(flat, flat, flat), in_specs=[VMEM] * 8,...]
    unnamed x8 -> x7, local copies, waits for them, and re-layouts: 4.76 us -> 3.46 us
where the time goes in v3:
time: 140 us
  Pallas kernels  136 us (97%)
  local copies, waits for them, and re-layouts  3.46 us (2%)
    pallas_call x1, Pallas kernels, per_device(): pl.pallas_call(solve, out_shape=(flat, flat, flat), in_specs=[VMEM] * 8,...  136 us
    unnamed x7, local copies, waits for them, and re-layouts  3.46 us

profile of v3, /device:TPU:1, one launch (start us, length us, event | category | flops | bytes accessed | tf_op | source)
XLA Modules:
  0.0 139.8 jit_solution(2965472040979086902)
XLA Ops:
  0.6 135.7 %shard_map.103 = (f32[16,4096]{1,0:T(8,128)}, f32[16,4096]{1,0:T(8,128)}, f32[16,4096]{1,0:T(8,128)}) custom-call(f32[16,4096]{1,0:T(8,128)} %coords.1, f32[16,4096]{1,0:T(8,128)} %x_in.1, f32[16,4096]{1,0:T(8,128)} %r_in.1, f32[16,4096]{1,0:T(8,128)} %p_in.1, s32[32,128]{1,0:T(8,128)} %bitcast.1, s32[2,256]{1,0:T(2,128)} %leaf_skel.1, s32[1,256]{1,0:T(1,128)} %local_skel.1, ...), custom_call_target="tpu_custom_call" | custom-call | tf_op jit(solution)/shard_map/pallas_call | solution.py:497
  136.3 0.0 copy-start.1
  136.3 1.7 %copy.14 = f32[16,4096]{1,0:T(8,128)} copy(f32[16,4096]{1,0:T(8,128)} %get-tuple-element.6) | data formatting | bytes 524288
  138.0 0.0 copy-done.1
  138.0 0.0 copy-start
  138.0 0.7 copy.15
  138.7 0.3 copy-done
  139.1 0.7 copy.16
Async XLA Ops:
  136.3 1.7 %copy-start.1 = (f32[16,4096]{1,0:T(8,128)S(1)}, f32[16,4096]{1,0:T(8,128)}, u32[]{:S(2)}) copy-start(f32[16,4096]{1,0:T(8,128)} %get-tuple-element.7) | copy-start | bytes 786436
  138.0 1.0 copy-start

commit v4 on v3

--- a/solution.py
+++ b/solution.py
@@ -108,8 +108,8 @@
 def solve(coords, x_in, r_in, p_in, order, leaf_skel, local_skel, upper, x_out, r_out, p_out,
           near_mat, lefts, rights, ut_hi, ut_lo, t_hi, t_lo, pts, vec, vsplit, image, q_ref, r_ref, p_ref, gain,
           digits, marks, inverse, skel, parent, state, cps,
-          points_out, points_in, coef_out, coef_in, sums_out, sums_in, middles, line_out, line_in, plane_in, tile_out, tile_in,
-          send_sem, recv_sem, sums_send, sums_recv, line_send, line_recv, plane_recv, tile_send, tile_recv):
+          points_out, points_in, coef_out, coef_in, sums_out, sums_in, middles, coefs, line_out, line_in, plane_out, plane_in,
+          send_sem, recv_sem, sums_send, sums_recv, line_send, line_recv, plane_send, plane_recv):
     me = lax.axis_index("leaf")
     rounds = 4
     line = 16
@@ -164,13 +164,13 @@
             for t in range(1, line)
         ]
 
-    def plane_copies():
+    def plane_copies(phase):
         return [
             pltpu.make_async_remote_copy(
-                src_ref=line_out,
-                dst_ref=plane_in.at[t - 1],
-                send_sem=line_send.at[t - 1],
-                recv_sem=plane_recv.at[t - 1],
+                src_ref=plane_out,
+                dst_ref=plane_in.at[phase, t - 1],
+                send_sem=plane_send.at[t - 1],
+                recv_sem=plane_recv.at[phase, t - 1],
                 device_id=(on_plane(t),),
                 device_id_type=MESH,
             )
@@ -179,20 +179,18 @@
 
     tile_lane = lax.broadcasted_iota(jnp.int32, (8, LANES), 1)
 
-    def to_tile(column):
-        return jnp.where(tile_lane == 0, column[0:8], jnp.where(tile_lane == 1, column[8:16], 0.0))
-
-    def from_tile(tile):
-        return jnp.concatenate([tile[:, 0:1], tile[:, 1:2]], axis=0)
-
-    def tile_copies(phase, n):
-        return copies(tile_out.at[n], tile_in.at[phase, n], tile_send.at[n], tile_recv.at[phase, n], n + 2)
-
-    def tile_sum(phase, n):
-        return (tile_out[n] + tile_in[phase, n, 0]) + (tile_in[phase, n, 1] + tile_in[phase, n, 2])
-
-    def line_sum(got):
-        parts = [line_out[...]] + [got[t] for t in range(line - 1)]
+    def to_tile(*columns):
+        tile = jnp.zeros((8, LANES), F32)
+        for n, column in enumerate(columns):
+            tile = jnp.where(tile_lane == 2 * n, column[0:8], tile)
+            tile = jnp.where(tile_lane == 2 * n + 1, column[8:16], tile)
+        return tile
+
+    def from_tile(tile, n=0):
+        return jnp.concatenate([tile[:, 2 * n : 2 * n + 1], tile[:, 2 * n + 1 : 2 * n + 2]], axis=0)
+
+    def line_sum(own, got):
+        parts = [own[...]] + [got[t] for t in range(line - 1)]
         while len(parts) > 1:
             parts = [a + b for a, b in zip(parts[0::2], parts[1::2])]
         return parts[0]
@@ -246,19 +244,17 @@
         parent[:, ob * LANES : (ob + 1) * LANES] = got
     pl.semaphore_wait(barrier, 2 * (line - 1))
 
-    def place_state():
-        sources = [block_of(r_in), block_of(p_in)]
-
+    def place_state(source, target):
         def body(group, carry):
             for n in range(4):
                 ob = group * 4 + n
                 span = pl.ds(pl.multiple_of(ob * LANES, LANES), LANES)
-                got = pick(sources, order[pl.ds(ob, 1), :], 0, blocks)
-                r_ref[:, span] = got[0]
-                vec[:, span] = got[1]
+                target[:, span] = pick([block_of(source)], order[pl.ds(ob, 1), :], 0, blocks)[0]
             return carry
 
         lax.fori_loop(0, blocks // 4, body, 0)
+
+    def invert():
         found = mm_t(digits[...], marks[...])
         inverse[...] = (found[0:blocks] * 32.0 + found[blocks : 2 * blocks]).astype(jnp.int32)
 
@@ -296,6 +292,12 @@
         for leaf in range(leaves):
             keep(local + leaf, softmax2(mm(skel_left[leaf], parent_right), 1))
         keep(local + 2, jnp.exp2(mm(skel_left[0], right_form(skel[1]))) * scale)
+
+    def make_gram():
+        for leaf in range(leaves):
+            high, low = ut_hi[leaf], ut_lo[leaf]
+            cross = mm_t(high, low)
+            keep(local + 3 + leaf, mm_t(high, high) + (cross + jnp.transpose(cross, (1, 0))))
 
     def make_round(g):
         base = g * PER_ROUND
@@ -315,7 +317,7 @@
                 keep(base + UP0 + n, softmax2(mm(mid_left[n], top_right), 1))
 
     beside = [
-        (place_state,),
+        (lambda: place_state(p_in, vec),),
         (make_near,),
         (lambda: make_basis(0), lambda: make_round(0)),
         (lambda: make_basis(1), lambda: make_round(1), make_local),
@@ -344,26 +346,51 @@
     q_ref[...] = jnp.zeros_like(q_ref)
     gain[...] = jnp.zeros_like(gain)
     state[0] = jnp.ones(state.shape[1:], F32)
-    state[1] = jnp.zeros(state.shape[1:], F32)
-    state[2] = jnp.zeros(state.shape[1:], F32)
+    for n in range(1, state.shape[0]):
+        state[n] = jnp.zeros(state.shape[1:], F32)
     lane = lax.broadcasted_iota(jnp.int32, (rhs, LANES), 1)
-
-    def near_product(leaf):
+    OF_V, OF_R, OF_P, OF_Q, OF_NEAR, DOWN = range(6)
+
+    def columns(leaf):
+        return slice(leaf * leaf_size, (leaf + 1) * leaf_size)
+
+    def leaf_up(ref, leaf):
+        part = stack3(ref[:, columns(leaf)])
+        return fold3(mm_t(part, ut_hi[leaf]) + mm_t(part, ut_lo[leaf]))
+
+    def near_product(leaf, first, last):
         def body(j, carry):
             inner = pl.ds(pl.multiple_of(j * rank, rank), rank)
             span = pl.ds(pl.multiple_of(leaf * leaf_size + j * rank, rank), rank)
-            wide = fold3(mm(vsplit[:, leaf * leaf_size : (leaf + 1) * leaf_size], near_mat[leaf, :, inner]))
+            wide = fold3(mm(vsplit[:, columns(leaf)], near_mat[leaf, :, inner]))
             image[:, span] = 0.5 * vec[:, span] + wide * scale
             return carry
 
-        lax.fori_loop(0, leaf_size // rank, body, 0)
+        lax.fori_loop(first, last, body, 0)
+
+    def finish():
+        alpha, beta, guess = (state[n, :, 0:1] for n in (3, 4, 2))
+        for leaf in range(leaves):
+            cols = columns(leaf)
+            part = stack3(coefs[DOWN, leaf])
+            full = image[:, cols] + fold3(mm(part, ut_hi[leaf]) + mm(part, ut_lo[leaf]))
+            p_new = vec[:, cols] + beta * p_ref[:, cols]
+            q_new = full + beta * q_ref[:, cols]
+            p_ref[:, cols] = p_new
+            q_ref[:, cols] = q_new
+            gain[:, cols] += alpha * p_new
+            r_new = r_ref[:, cols] - alpha * q_new
+            r_ref[:, cols] = r_new
+            vec[:, cols] = r_new + guess * p_new
+
+    for leaf in range(leaves):
+        coefs[OF_V, leaf] = leaf_up(vec, leaf)
+        coefs[OF_P, leaf] = jnp.zeros(coefs.shape[2:], F32)
+        coefs[OF_Q, leaf] = jnp.zeros(coefs.shape[2:], F32)
+    chunks = leaf_size // rank
 
     def iteration(k, carry):
-        vsplit[...] = stack3(vec[...])
-        leaf_coef = []
-        for leaf in range(leaves):
-            part = vsplit[:, leaf * leaf_size : (leaf + 1) * leaf_size]
-            leaf_coef.append(fold3(mm_t(part, ut_hi[leaf]) + mm_t(part, ut_lo[leaf])))
+        leaf_coef = [coefs[OF_V, leaf] for leaf in range(leaves)]
         wide = [stack3(x) for x in leaf_coef]
         coef = times(wide[0], local) + times(wide[1], local + 1)
         last = None
@@ -375,33 +402,53 @@
                 c.start()
             if g == 0:
                 leaf_cp = [times_t(wide[1], local + 2), times(wide[0], local + 2)]
-                sums = jnp.where(lane == 0, row_dot(r_ref[...], r_ref[...]), 0.0)
-                sums = jnp.where(lane == 1, row_dot(vec[...], q_ref[...]), sums)
-                sums = jnp.where(lane == 3, row_dot(r_ref[...], vec[...]), sums)
-                sums = jnp.where(lane == 4, row_dot(vec[...], vec[...]), sums)
-                sums = jnp.where(lane == 2, 2.0 * row_dot(leaf_coef[0], leaf_cp[0]), sums)
+                sums = jnp.where(lane == 2, 2.0 * row_dot(leaf_coef[0], leaf_cp[0]), 0.0)
             else:
                 sums = last()
             sums_out[g] = sums
             sum_sends = copies(sums_out.at[g], sums_in.at[k, g], sums_send.at[g], sums_recv.at[k, g], g)
             for c in sum_sends:
                 c.start()
-            if g < leaves:
-                near_product(g)
+            if g == 0:
+                pl.when(k > 0)(finish)
+                pl.when(k == 0)(lambda: place_state(r_in, r_ref))
+                vsplit[...] = stack3(vec[...])
+                near_product(0, 0, chunks // 4)
             if g == 1:
-                line_out[...] = to_tile(row_dot(vec[...], image[...]))
+                near_product(0, chunks // 4, chunks)
+                near_product(1, 0, chunks)
+                line_out[...] = to_tile(
+                    row_dot(vec[...], image[...]),
+                    row_dot(r_ref[...], r_ref[...]),
+                    row_dot(vec[...], q_ref[...]),
+                    row_dot(r_ref[...], vec[...]),
+                    row_dot(vec[...], vec[...]),
+                )
                 side = line_copies(k)
-            else:
-                if g > 1:
-                    for c in side:
-                        c.wait()
-                    tile_out[g - 2] = line_sum(line_in.at[k]) if g == 2 else tile_sum(k, 0)
-                    side = tile_copies(k, g - 2)
-            if g > 0:
                 for c in side:
                     c.start()
-            if g in (1, 2):
-                pl.when(k == 0)(lambda g=g: make_round(g + 1))
+            if g == 2:
+                for leaf in range(leaves):
+                    coefs[OF_NEAR, leaf] = leaf_up(image, leaf)
+            if g == 3:
+                for c in side:
+                    c.wait()
+                plane_out[...] = line_sum(line_out, line_in.at[k])
+                side = plane_copies(k)
+                for c in side:
+                    c.start()
+            if g > 0:
+
+                @pl.when(k == 0)
+                def _(g=g):
+                    if g < 3:
+                        make_round(g + 1)
+                    else:
+                        make_gram()
+                        invert()
+                        for leaf in range(leaves):
+                            coefs[OF_R, leaf] = leaf_up(r_ref, leaf)
+
             for c in sends:
                 c.wait()
             got = [coef] + [coef_in[k, g, t] for t in range(3)]
@@ -428,33 +475,33 @@
         for u in range(2 * rounds - 2, -1, -1):
             down = cps[u] + times_t(stack3(down), (u // 2) * PER_ROUND + (UP0 if u % 2 else OWN0))
         down_wide = stack3(down)
+        image_coef = []
         for leaf in range(leaves):
-            cols = slice(leaf * leaf_size, (leaf + 1) * leaf_size)
-            part = stack3(leaf_cp[leaf] + times_t(down_wide, local + leaf))
-            image[:, cols] += fold3(mm(part, ut_hi[leaf]) + mm(part, ut_lo[leaf]))
+            leaf_down = leaf_cp[leaf] + times_t(down_wide, local + leaf)
+            coefs[DOWN, leaf] = leaf_down
+            image_coef.append(coefs[OF_NEAR, leaf] + times(stack3(leaf_down), local + 3 + leaf))
         for c in side:
             c.wait()
-        near = from_tile(tile_sum(k, 1))
-        fresh = sums[:, 0:1]
-        cross = sums[:, 1:2]
+        tile = line_sum(plane_out, plane_in.at[k])
+        near, fresh, cross, with_v, of_v = (from_tile(tile, n) for n in range(5))
         beta = fresh / state[0, :, 0:1] - state[2, :, 0:1]
-        guess = jnp.where(k == 0, 1.0 + (fresh - 2.0 * sums[:, 3:4]) / sums[:, 4:5], 0.0)
-        state[2] = jnp.broadcast_to(guess, (rhs, LANES))
+        guess = jnp.where(k == 0, 1.0 + (fresh - 2.0 * with_v) / of_v, 0.0)
         curve = (sums[:, 2:3] + near) + 2.0 * beta * cross + beta * beta * state[1, :, 0:1]
         alpha = fresh / curve
-        state[0] = jnp.broadcast_to(fresh, (rhs, LANES))
-        state[1] = jnp.broadcast_to(curve, (rhs, LANES))
-        p_new = vec[...] + beta * p_ref[...]
-        q_new = image[...] + beta * q_ref[...]
-        p_ref[...] = p_new
-        q_ref[...] = q_new
-        gain[...] += alpha * p_new
-        r_new = r_ref[...] - alpha * q_new
-        r_ref[...] = r_new
-        vec[...] = r_new + guess * p_new
+        for n, column in enumerate((fresh, curve, guess, alpha, beta)):
+            state[n] = jnp.broadcast_to(column, (rhs, LANES))
+        for leaf in range(leaves):
+            p_coef = coefs[OF_V, leaf] + beta * coefs[OF_P, leaf]
+            q_coef = image_coef[leaf] + beta * coefs[OF_Q, leaf]
+            r_coef = coefs[OF_R, leaf] - alpha * q_coef
+            coefs[OF_P, leaf] = p_coef
+            coefs[OF_Q, leaf] = q_coef
+            coefs[OF_R, leaf] = r_coef
+            coefs[OF_V, leaf] = r_coef + guess * p_coef
         return carry
 
     lax.fori_loop(0, ITERS, iteration, 0)
+    finish()
 
     sources = [block_of(gain), block_of(r_ref), block_of(p_ref)]
 
@@ -475,14 +522,14 @@
     lax.fori_loop(0, blocks // 8, restore, 0)
     for c in sends:
         c.wait()
-    line_out[...] = line_sum(line_in.at[ITERS])
-    sends = plane_copies()
+    plane_out[...] = line_sum(line_out, line_in.at[ITERS])
+    sends = plane_copies(ITERS)
     for c in sends:
         c.start()
     lax.fori_loop(blocks // 8, blocks // 4, restore, 0)
     for c in sends:
         c.wait()
-    tile = line_sum(plane_in)
+    tile = line_sum(plane_out, plane_in.at[ITERS])
     p_out[...] = r_out[...] + from_tile(tile) / state[0, :, 0:1] * p_out[...]
 
 
@@ -493,7 +540,7 @@
     leaf_size = count // leaves
     blocks = count // LANES
     flat = jax.ShapeDtypeStruct((rhs, count), F32)
-    slots = 4 * PER_ROUND + 3
+    slots = 4 * PER_ROUND + 5
     return pl.pallas_call(
         solve,
         out_shape=(flat, flat, flat),
@@ -520,7 +567,7 @@
             pltpu.VMEM((blocks, LANES), jnp.int32),
             pltpu.VMEM((leaves, dims, rank), F32),
             pltpu.VMEM((dims, rank), F32),
-            pltpu.VMEM((3, rhs, LANES), F32),
+            pltpu.VMEM((5, rhs, LANES), F32),
             pltpu.VMEM((8, rhs, rank), F32),
             pltpu.VMEM((4, dims + 8, rank), F32),
             pltpu.VMEM((4, 3, dims + 8, rank), F32),
@@ -529,11 +576,11 @@
             pltpu.VMEM((4, rhs, LANES), F32),
             pltpu.VMEM((ITERS, 4, 3, rhs, LANES), F32),
             pltpu.VMEM((4, 2, dims, rank), F32),
+            pltpu.VMEM((6, leaves, rhs, rank), F32),
             pltpu.VMEM((8, LANES), F32),
             pltpu.VMEM((ITERS + 1, 15, 8, LANES), F32),
-            pltpu.VMEM((15, 8, LANES), F32),
-            pltpu.VMEM((2, 8, LANES), F32),
-            pltpu.VMEM((ITERS, 2, 3, 8, LANES), F32),
+            pltpu.VMEM((8, LANES), F32),
+            pltpu.VMEM((ITERS + 1, 15, 8, LANES), F32),
             pltpu.SemaphoreType.DMA((4, 3)),
             pltpu.SemaphoreType.DMA((ITERS + 1, 4, 3)),
             pltpu.SemaphoreType.DMA((4, 3)),
@@ -541,8 +588,7 @@
             pltpu.SemaphoreType.DMA((15,)),
             pltpu.SemaphoreType.DMA((ITERS + 1, 15)),
             pltpu.SemaphoreType.DMA((15,)),
-            pltpu.SemaphoreType.DMA((2, 3)),
-            pltpu.SemaphoreType.DMA((ITERS, 2, 3)),
+            pltpu.SemaphoreType.DMA((ITERS + 1, 15)),
         ],
         compiler_params=pltpu.CompilerParams(
             vmem_limit_bytes=56 * 1024 * 1024, collective_id=0, has_side_effects=True

time: 140 us -> 132 us (0.943)
  Pallas kernels: 136 us -> 128 us
    pallas_call x1, Pallas kernels: 136 us -> 128 us  [per_device(): pl.pallas_call(solve, out_shape=(flat, flat, flat), in_specs=[VMEM] * 8,...]
where the time goes in v4:
time: 132 us
  Pallas kernels  128 us (97%)
  local copies, waits for them, and re-layouts  3.46 us (3%)
    pallas_call x1, Pallas kernels, per_device(): pl.pallas_call(solve, out_shape=(flat, flat, flat), in_specs=[VMEM] * 8,...  128 us
    unnamed x7, local copies, waits for them, and re-layouts  3.46 us

profile of v4, /device:TPU:1, one launch (start us, length us, event | category | flops | bytes accessed | tf_op | source)
XLA Modules:
  0.0 132.0 jit_solution(11737606636297863493)
XLA Ops:
  0.6 127.8 %shard_map.103 = (f32[16,4096]{1,0:T(8,128)}, f32[16,4096]{1,0:T(8,128)}, f32[16,4096]{1,0:T(8,128)}) custom-call(f32[16,4096]{1,0:T(8,128)} %coords.1, f32[16,4096]{1,0:T(8,128)} %x_in.1, f32[16,4096]{1,0:T(8,128)} %r_in.1, f32[16,4096]{1,0:T(8,128)} %p_in.1, s32[32,128]{1,0:T(8,128)} %bitcast.1, s32[2,256]{1,0:T(2,128)} %leaf_skel.1, s32[1,256]{1,0:T(1,128)} %local_skel.1, ...), custom_call_target="tpu_custom_call" | custom-call | tf_op jit(solution)/shard_map/pallas_call | solution.py:544
  128.5 0.0 copy-start.1
  128.5 1.7 %copy.14 = f32[16,4096]{1,0:T(8,128)} copy(f32[16,4096]{1,0:T(8,128)} %get-tuple-element.6) | data formatting | bytes 524288
  130.2 0.0 copy-done.1
  130.2 0.0 copy-start
  130.2 0.7 copy.15
  130.9 0.3 copy-done
  131.3 0.7 copy.16
Async XLA Ops:
  128.5 1.7 %copy-start.1 = (f32[16,4096]{1,0:T(8,128)S(1)}, f32[16,4096]{1,0:T(8,128)}, u32[]{:S(2)}) copy-start(f32[16,4096]{1,0:T(8,128)} %get-tuple-element.7) | copy-start | bytes 786436
  130.2 1.0 copy-start

commit v5 on v4

--- a/solution.py
+++ b/solution.py
@@ -105,7 +105,13 @@
     return jnp.sum(a * b, axis=1, keepdims=True)
 
 
-def solve(coords, x_in, r_in, p_in, order, leaf_skel, local_skel, upper, x_out, r_out, p_out,
+def finish_state(x_in, gain, r_in, p_in, ratio, x_out, r_out, p_out):
+    x_out[...] = x_in[...] + gain[...]
+    r_out[...] = r_in[...]
+    p_out[...] = r_in[...] + ratio[:, 0:1] * p_in[...]
+
+
+def solve(coords, r_in, p_in, order, leaf_skel, local_skel, upper, x_out, r_out, p_out, ratio,
           near_mat, lefts, rights, ut_hi, ut_lo, t_hi, t_lo, pts, vec, vsplit, image, q_ref, r_ref, p_ref, gain,
           digits, marks, inverse, skel, parent, state, cps,
           points_out, points_in, coef_out, coef_in, sums_out, sums_in, middles, coefs, line_out, line_in, plane_out, plane_in,
@@ -328,8 +334,8 @@
         points_out[g, 0:16, :] = own
         points_out[g, 16:24, :] = jnp.broadcast_to(upper[u].astype(F32), (8, rank))
         sends = copies(points_out.at[g], points_in.at[g], send_sem.at[g], recv_sem.at[0, g], g)
-        for c in sends:
-            c.start()
+        for t in (2, 3, 1):
+            sends[t - 1].start()
         for work in beside[g]:
             work()
         for c in sends:
@@ -398,8 +404,8 @@
             base = g * PER_ROUND
             coef_out[g] = coef
             sends = copies(coef_out.at[g], coef_in.at[k, g], send_sem.at[g], recv_sem.at[1 + k, g], g)
-            for c in sends:
-                c.start()
+            for t in (2, 3, 1):
+                sends[t - 1].start()
             if g == 0:
                 leaf_cp = [times_t(wide[1], local + 2), times(wide[0], local + 2)]
                 sums = jnp.where(lane == 2, 2.0 * row_dot(leaf_coef[0], leaf_cp[0]), 0.0)
@@ -449,15 +455,22 @@
                         for leaf in range(leaves):
                             coefs[OF_R, leaf] = leaf_up(r_ref, leaf)
 
-            for c in sends:
-                c.wait()
-            got = [coef] + [coef_in[k, g, t] for t in range(3)]
-            wide = [stack3(x) for x in got]
-            mid0 = times(wide[0], base + OWN0) + times(wide[1], base + OWN1)
-            mid1 = times(wide[2], base + OWN2) + times(wide[3], base + OWN3)
+            got = [coef] + [None] * 3
+            wide = [stack3(coef)] + [None] * 3
+            moved = [times(wide[0], base + OWN0)] + [None] * 3
+            for t in (1, 3, 2):
+                sends[t - 1].wait()
+                got[t] = coef_in[k, g, t - 1]
+                wide[t] = stack3(got[t])
+                moved[t] = times(wide[t], base + OWN0 + t)
+                if t == 1:
+                    mid0 = moved[0] + moved[1]
+                    if g + 1 < rounds:
+                        up0 = times(stack3(mid0), base + UP0)
+            mid1 = moved[2] + moved[3]
             mid1_wide = stack3(mid1)
             if g + 1 < rounds:
-                coef = times(stack3(mid0), base + UP0) + times(mid1_wide, base + UP1)
+                coef = up0 + times(mid1_wide, base + UP1)
 
             def last(g=g, base=base, got=got, wide=wide, mid0=mid0, mid1_wide=mid1_wide, sums=sums, sent=sum_sends):
                 low_cp = times(wide[1], base + SIB)
@@ -510,7 +523,7 @@
             ob = group * 4 + n
             span = pl.ds(pl.multiple_of(ob * LANES, LANES), LANES)
             got = pick(sources, inverse[pl.ds(ob, 1), :], 0, blocks)
-            x_out[:, span] = x_in[:, span] + got[0]
+            x_out[:, span] = got[0]
             r_out[:, span] = got[1]
             p_out[:, span] = got[2]
         return carry
@@ -530,7 +543,7 @@
     for c in sends:
         c.wait()
     tile = line_sum(plane_out, plane_in.at[ITERS])
-    p_out[...] = r_out[...] + from_tile(tile) / state[0, :, 0:1] * p_out[...]
+    ratio[...] = jnp.broadcast_to(from_tile(tile) / state[0, :, 0:1], ratio.shape)
 
 
 def per_device(coords, solution, residual, direction, order, leaf_skel, local_skel, upper_skel):
@@ -541,11 +554,11 @@
     blocks = count // LANES
     flat = jax.ShapeDtypeStruct((rhs, count), F32)
     slots = 4 * PER_ROUND + 5
-    return pl.pallas_call(
+    gain, resid, search, ratio = pl.pallas_call(
         solve,
-        out_shape=(flat, flat, flat),
-        in_specs=[VMEM] * 8,
-        out_specs=(VMEM,) * 3,
+        out_shape=(flat, flat, flat, jax.ShapeDtypeStruct((rhs, LANES), F32)),
+        in_specs=[VMEM] * 7,
+        out_specs=(VMEM,) * 4,
         scratch_shapes=[
             pltpu.VMEM((leaves, leaf_size, leaf_size), BF16),
             pltpu.VMEM((leaves, leaf_size, LANES), BF16),
@@ -595,7 +608,6 @@
         ),
     )(
         coords,
-        solution,
         residual,
         direction,
         order.reshape(blocks, LANES),
@@ -603,6 +615,12 @@
         local_skel,
         upper_skel,
     )
+    return pl.pallas_call(
+        finish_state,
+        out_shape=(flat, flat, flat),
+        in_specs=[VMEM] * 5,
+        out_specs=(VMEM,) * 3,
+    )(solution, gain, resid, search, ratio)
 
 
 def solution(mesh):

time: 132 us -> 129 us (0.977)
  local copies, waits for them, and re-layouts: 3.46 us -> 0 us
    unnamed x7 -> x0, local copies, waits for them, and re-layouts: 3.46 us -> none
    pallas_call x1 -> x2, Pallas kernels: 128 us -> 129 us  [the longest x1 127 us: per_device(): pl.pallas_call(solve, out_shape=(flat, flat, flat, jax.ShapeDtypeStruct((...]
where the time goes in v5:
time: 129 us
  Pallas kernels  129 us (100%)
    pallas_call x1, Pallas kernels, per_device(): pl.pallas_call(solve, out_shape=(flat, flat, flat, jax.ShapeDtypeStruct((...  127 us

profile of v5, /device:TPU:1, one launch (start us, length us, event | category | flops | bytes accessed | tf_op | source)
XLA Modules:
  0.0 129.4 jit_solution(9781593736091544767)
XLA Ops:
  0.6 126.6 %shard_map.103 = (f32[16,4096]{1,0:T(8,128)}, f32[16,4096]{1,0:T(8,128)}, f32[16,4096]{1,0:T(8,128)}, f32[16,128]{1,0:T(8,128)}) custom-call(f32[16,4096]{1,0:T(8,128)} %coords.1, f32[16,4096]{1,0:T(8,128)} %r_in.1, f32[16,4096]{1,0:T(8,128)} %p_in.1, s32[32,128]{1,0:T(8,128)} %bitcast.1, s32[2,256]{1,0:T(2,128)} %leaf_skel.1, s32[1,256]{1,0:T(1,128)} %local_skel.1, ...), custom_call_target="tpu_custom_call" | custom-call | tf_op jit(solution)/shard_map/pallas_call | solution.py:557
  127.3 2.1 %shard_map.104 = (f32[16,4096]{1,0:T(8,128)}, f32[16,4096]{1,0:T(8,128)}, f32[16,4096]{1,0:T(8,128)}) custom-call(f32[16,4096]{1,0:T(8,128)} %x_in.1, f32[16,4096]{1,0:T(8,128)} %get-tuple-element.7.gain, f32[16,4096]{1,0:T(8,128)} %get-tuple-element.8.r_in, f32[16,4096]{1,0:T(8,128)} %get-tuple-element.9.p_in, f32[16,128]{1,0:T(8,128)} %get-tuple-element.10.ratio), custom_call_target="tpu_custom_call" | custom-call | tf_op jit(solution)/shard_map/pallas_call | solution.py:618

commit v6 on v5

--- a/solution.py
+++ b/solution.py
@@ -17,6 +17,9 @@
 
 OWN0, OWN1, OWN2, OWN3, UP0, UP1, SIB, COUSIN, UNCLE = range(9)
 PER_ROUND = 9
+
+LINE_ORDER = (8, 9, 10, 11, 6, 7, 14, 15, 4, 5, 12, 13, 2, 3, 1)
+PLANE_ORDER = (10, 6, 14, 9, 11, 5, 7, 13, 15, 2, 8, 1, 3, 4, 12)
 
 
 def pick(sources, index_row, first_block, block_count):
@@ -167,7 +170,7 @@
                 device_id=(on_line(t),),
                 device_id_type=MESH,
             )
-            for t in range(1, line)
+            for t in LINE_ORDER
         ]
 
     def plane_copies(phase):
@@ -180,7 +183,7 @@
                 device_id=(on_plane(t),),
                 device_id_type=MESH,
             )
-            for t in range(1, line)
+            for t in PLANE_ORDER
         ]
 
     tile_lane = lax.broadcasted_iota(jnp.int32, (8, LANES), 1)

time: 129 us -> 129 us (level)
  no operation moved by 1% of the time
where the time goes in v6:
time: 129 us
  Pallas kernels  128 us (99%)
    pallas_call x1, Pallas kernels, per_device(): pl.pallas_call(solve, out_shape=(flat, flat, flat, jax.ShapeDtypeStruct((...  126 us

profile of v6, /device:TPU:1, one launch (start us, length us, event | category | flops | bytes accessed | tf_op | source)
XLA Modules:
  0.0 129.1 jit_solution(11363971640606608580)
XLA Ops:
  0.6 126.4 %shard_map.103 = (f32[16,4096]{1,0:T(8,128)}, f32[16,4096]{1,0:T(8,128)}, f32[16,4096]{1,0:T(8,128)}, f32[16,128]{1,0:T(8,128)}) custom-call(f32[16,4096]{1,0:T(8,128)} %coords.1, f32[16,4096]{1,0:T(8,128)} %r_in.1, f32[16,4096]{1,0:T(8,128)} %p_in.1, s32[32,128]{1,0:T(8,128)} %bitcast.1, s32[2,256]{1,0:T(2,128)} %leaf_skel.1, s32[1,256]{1,0:T(1,128)} %local_skel.1, ...), custom_call_target="tpu_custom_call" | custom-call | tf_op jit(solution)/shard_map/pallas_call | solution.py:560
  127.0 2.1 %shard_map.104 = (f32[16,4096]{1,0:T(8,128)}, f32[16,4096]{1,0:T(8,128)}, f32[16,4096]{1,0:T(8,128)}) custom-call(f32[16,4096]{1,0:T(8,128)} %x_in.1, f32[16,4096]{1,0:T(8,128)} %get-tuple-element.7.gain, f32[16,4096]{1,0:T(8,128)} %get-tuple-element.8.r_in, f32[16,4096]{1,0:T(8,128)} %get-tuple-element.9.p_in, f32[16,128]{1,0:T(8,128)} %get-tuple-element.10.ratio), custom_call_target="tpu_custom_call" | custom-call | tf_op jit(solution)/shard_map/pallas_call | solution.py:621
